TPU v7x, 512 devices: a whole 4x8x8 slice. The times are simulated.
512 devices in a mesh: tm: 64 (over z, x, core), runs: 8 (over y).
Axes of the slice: x: 4, y: 8, z: 8, core: 2. Of those that a mesh axis runs over, the one named last changes fastest.
Arguments:
- samples: float32 [16, 131072, 128], P('runs', 'tm'), may hold values from -24 to 24, as said below
- cohesion: int32 [16], replicated, may hold values from 0 to 3
- rolling: int32 [16], replicated, may hold values from 0 to 3
Outputs:
- level_mean: float32 [4, 64, 2, 128, 128], P(None, 'tm')
- level_spread: float32 [4, 64, 128, 128], P(None, 'tm')
- roll_mean: float32 [4, 64, 2, 128, 128], P(None, 'tm')
Inputs may be any that keep to these rules, and one draw needn't show every extreme that they name: `samples`: each channel of each run is filtered noise with a gain of its own and correlation with the next channel.
All inputs are finite; a program needn't handle non-finite values.
Results may differ from a plain program's by a relative error of at most 0.00016.
Values sent between devices are 32-bit elements; how exact they have to be, the bound alone decides.
No kernel may reach another device: no remote copies, remote signals or barrier semaphores. Data moves between devices by JAX's collectives and lax.ppermute only.
A program may use at most 64 MiB of HBM per device.

v0:
```python
import functools
import math

import jax
import jax.numpy as jnp
import ml_dtypes
import numpy as np
from jax import lax
from jax.experimental import pallas as pl
from jax.experimental.pallas import tpu as pltpu
from jax.sharding import PartitionSpec as P

CH = 128
BIN = 1024
NC = 4
NQ = 4
TOTAL = 131072
RUNS = 16
NB = 64
T1 = 512
T2 = 256

NT = (((1,), (1,)), ((), ()))
MIB = 1 << 20


def split_table(table):
    high = table.astype(ml_dtypes.bfloat16)
    low = (table - high.astype(np.float64)).astype(ml_dtypes.bfloat16)
    return high, low


@functools.lru_cache(maxsize=None)
def tables():
    k1 = np.arange(256)
    t1 = np.arange(T1)
    angle = 2.0 * np.pi * (k1[:, None] * t1[None, :] % T1) / T1
    sine = -np.sin(angle)
    sine[0] = np.cos(np.pi * (t1 % 2))
    first = np.concatenate([np.cos(angle), sine], axis=0)
    t2 = np.arange(T2)
    turn = 2.0 * np.pi * (k1[:, None] * t2[None, :]) / TOTAL
    cos_t, sin_t = np.cos(turn), np.sin(turn)
    second = np.zeros((NB, 2, 4, 2, T2))
    edge = np.zeros((NB, 2, 4, 2, T2))
    for band in range(NB):
        for m, (k2, sign) in enumerate(
            [(2 * band, 1.0), (2 * band + 1, 1.0), (255 - 2 * band, -1.0), (254 - 2 * band, -1.0)]
        ):
            a = 2.0 * np.pi * (k2 * t2 % T2) / T2
            second[band, 0, m, 0] = np.cos(a)
            second[band, 0, m, 1] = np.sin(a)
            second[band, 1, m, 0] = -sign * np.sin(a)
            second[band, 1, m, 1] = sign * np.cos(a)
        for m in range(4):
            half = m // 2
            a = 2.0 * np.pi * ((2 * (2 * band + m % 2) + half) * t2 % 512) / 512
            edge[band, 0, m, half] = np.cos(a)
            edge[band, 1, m, half] = -np.sin(a)
    second = second.reshape(NB * 8, 2 * T2)
    edge = edge.reshape(NB * 8, 2 * T2)
    t = np.arange(TOTAL).reshape(T1, T2)
    window = 0.5 - 0.5 * np.cos(2.0 * np.pi * t / TOTAL)
    first_h, first_l = split_table(first)
    second_h, second_l = split_table(second)
    edge_h, edge_l = split_table(edge)
    return (
        window.astype(np.float32),
        cos_t.astype(np.float32),
        sin_t.astype(np.float32),
        first_h,
        first_l,
        second_h,
        second_l,
        edge_h,
        edge_l,
    )


def split(value):
    high = value.astype(jnp.bfloat16)
    low = (value - high.astype(jnp.float32)).astype(jnp.bfloat16)
    return high, low


def dot(a, b):
    return jnp.dot(a, b, preferred_element_type=jnp.float32)


def dot_nt(a, b):
    return lax.dot_general(a, b, NT, preferred_element_type=jnp.float32)


def pack_kernel(x_ref, o_ref, turned):
    for u in range(8):
        turned[u * 128 : (u + 1) * 128, :] = x_ref[0, u, 0].T
    for ch in range(CH):
        o_ref[ch % 64, ch // 64, 0, 0] = turned[pl.ds(ch, 8, stride=128), :]


def pack(samples):
    x = samples.reshape(2, 8, 2, 128, CH)
    return pl.pallas_call(
        pack_kernel,
        grid=(2, 2),
        in_specs=[pl.BlockSpec((1, 8, 1, 128, CH), lambda r, h: (r, 0, h, 0, 0))],
        out_specs=pl.BlockSpec((64, 2, 1, 1, 8, 128), lambda r, h: (0, 0, r, h, 0, 0)),
        out_shape=jax.ShapeDtypeStruct((64, 2, 2, 2, 8, 128), jnp.float32),
        scratch_shapes=[pltpu.VMEM((1024, 128), jnp.float32)],
        compiler_params=pltpu.CompilerParams(vmem_limit_bytes=16 * MIB),
        name="pack",
    )(x)


def dft_kernel(x_ref, w_ref, c_ref, s_ref, fh_ref, fl_ref, sh_ref, sl_ref, eh_ref, el_ref, o_ref):
    halves = [x_ref[:, 0, 0, h].reshape(T1, 128) for h in range(2)]
    x = jnp.concatenate(halves, axis=1) * w_ref[...]
    xh, xl = split(x)
    fh = fh_ref[...]
    a = dot(fh, xh) + dot(fh, xl) + dot(fl_ref[...], xh)
    a_re, a_im = a[:256], a[256:]
    c, s = c_ref[...], s_ref[...]
    b = jnp.concatenate([a_re * c + a_im * s, a_im * c - a_re * s], axis=1)
    first_row = lax.broadcasted_iota(jnp.int32, (256, 512), 0) == 0
    eh, el = split(jnp.where(first_row[:128], b[:128], 0.0))
    bh, bl = split(jnp.where(first_row, 0.0, b))
    sh = sh_ref[...]
    o = dot_nt(sh, bh) + dot_nt(sh, bl) + dot_nt(sl_ref[...], bh)
    edge = eh_ref[...]
    e = dot_nt(edge, eh) + dot_nt(edge, el) + dot_nt(el_ref[...], eh)
    o_ref[:, 0, 0] = (o[:, :128] + e).reshape(NB, 8, 128)
    o_ref[:, 0, 1] = o[:, 128:].reshape(NB, 8, 128)


def dft(x):
    consts = [jnp.asarray(t) for t in tables()]
    whole = [
        pl.BlockSpec(t.shape, lambda i: (0, 0), pipeline_mode=pl.Buffered(1)) for t in consts
    ]
    return pl.pallas_call(
        dft_kernel,
        grid=(4,),
        in_specs=[pl.BlockSpec((64, 1, 1, 2, 8, 128), lambda i: (0, i // 2, i % 2, 0, 0, 0))]
        + whole,
        out_specs=pl.BlockSpec((NB, 1, 2, 8, 128), lambda i: (0, i, 0, 0, 0)),
        out_shape=jax.ShapeDtypeStruct((NB, 4, 2, 8, 128), jnp.float32),
        compiler_params=pltpu.CompilerParams(vmem_limit_bytes=32 * MIB),
        name="dft",
    )(x, *consts)


def cross_kernel(x_ref, o_ref, *, scale):
    row = lax.broadcasted_iota(jnp.int32, (CH, CH), 0)
    col = lax.broadcasted_iota(jnp.int32, (CH, CH), 1)
    for r in range(2):
        parts = []
        for part in range(2):
            for c in range(2):
                cols = [
                    x_ref[pl.ds((c * 2 + r) * 16 + half * 8 + part * 4 + m, 64, stride=64), :]
                    for m in range(4)
                    for half in range(2)
                ]
                parts.append(jnp.concatenate(cols, axis=1))
        v = jnp.concatenate(parts, axis=0)
        vh, vl = split(v)
        mixed = dot_nt(vh, vl)
        g = dot_nt(vh, vh) + (mixed + mixed.T)
        real = g[:CH, :CH] + g[CH:, CH:]
        imag = g[CH:, :CH] - g[:CH, CH:]
        packed = jnp.where(row >= col, real, imag) * scale
        for y in range(8):
            o_ref[y, r] = packed


def cross(x):
    scale = 1.0 / (0.375 * BIN * TOTAL)
    return pl.pallas_call(
        functools.partial(cross_kernel, scale=scale),
        in_specs=[pl.BlockSpec(memory_space=pltpu.VMEM)],
        out_specs=pl.BlockSpec(memory_space=pltpu.VMEM),
        out_shape=jax.ShapeDtypeStruct((8, 2, CH, CH), jnp.float32),
        compiler_params=pltpu.CompilerParams(vmem_limit_bytes=32 * MIB),
        name="cross",
    )(x.reshape(64 * 64, 128))


def moments_kernel(lev_ref, roll_ref, x_ref, lm_ref, sp_ref, rm_ref, sums, rolls, squares):
    row = lax.broadcasted_iota(jnp.int32, (CH, CH), 0)
    col = lax.broadcasted_iota(jnp.int32, (CH, CH), 1)
    sums[...] = jnp.zeros_like(sums)
    rolls[...] = jnp.zeros_like(rolls)
    squares[...] = jnp.zeros_like(squares)

    def unpack(m):
        t = m.T
        real = jnp.where(row >= col, m, t)
        imag = jnp.where(row < col, m, jnp.where(row > col, -t, 0.0))
        return real, imag

    def count(ref, level):
        total = jnp.int32(0)
        for r in range(RUNS):
            total += (ref[r] == level).astype(jnp.int32)
        return jnp.maximum(total, 1).astype(jnp.float32)

    for r in range(RUNS):
        value = x_ref[r]
        sums[lev_ref[r]] += value
        rolls[roll_ref[r]] += value
    for l in range(NC):
        mean = sums[l] / count(lev_ref, l)
        sums[l] = mean
        real, imag = unpack(mean)
        lm_ref[l, 0, 0] = real
        lm_ref[l, 0, 1] = imag
    for q in range(NQ):
        real, imag = unpack(rolls[q] / count(roll_ref, q))
        rm_ref[q, 0, 0] = real
        rm_ref[q, 0, 1] = imag
    for r in range(RUNS):
        level = lev_ref[r]
        offset = x_ref[r] - sums[level]
        squares[level] += offset * offset
    for l in range(NC):
        s = squares[l]
        sp_ref[l, 0] = BIN * jnp.where(row == col, s, s + s.T)


def moments(cohesion, rolling, x):
    vmem = pl.BlockSpec(memory_space=pltpu.VMEM)
    smem = pl.BlockSpec(memory_space=pltpu.SMEM)
    return pl.pallas_call(
        moments_kernel,
        in_specs=[smem, smem, vmem],
        out_specs=(vmem, vmem, vmem),
        out_shape=(
            jax.ShapeDtypeStruct((NC, 1, 2, CH, CH), jnp.float32),
            jax.ShapeDtypeStruct((NC, 1, CH, CH), jnp.float32),
            jax.ShapeDtypeStruct((NQ, 1, 2, CH, CH), jnp.float32),
        ),
        scratch_shapes=[pltpu.VMEM((4, CH, CH), jnp.float32)] * 3,
        compiler_params=pltpu.CompilerParams(vmem_limit_bytes=16 * MIB),
        name="moments",
    )(cohesion, rolling, x.reshape(RUNS, CH, CH))


def exchange(x, axis):
    return lax.all_to_all(x, axis, split_axis=0, concat_axis=0, tiled=True)


def per_device(samples, cohesion, rolling):
    series = exchange(pack(samples).reshape(64, 64, 128), "tm")
    bins = dft(series.reshape(64, 2, 2, 2, 8, 128))
    band = exchange(bins.reshape(64, 64, 128), "tm")
    gathered = exchange(cross(band), "runs")
    return moments(cohesion, rolling, gathered)


def solution(mesh):
    return jax.shard_map(
        per_device,
        mesh=mesh,
        in_specs=(P("runs", "tm", None), P(), P()),
        out_specs=(
            P(None, "tm", None, None, None),
            P(None, "tm", None, None),
            P(None, "tm", None, None, None),
        ),
        check_vma=False,
    )
```

profile of v0, /device:TPU:4, one launch (start us, length us, event | category | flops | bytes accessed | tf_op | source)
XLA Modules:
  0.0 171.5 jit_solution(6233166520314087561)
XLA Ops:
  0.6 0.0 copy-start
  0.6 1.6 copy-done
  2.2 2.4 %pack.1 = f32[64,2,2,2,8,128]{5,4,3,2,1,0:T(8,128)S(1)} custom-call(f32[2,8,2,128,128]{4,3,2,1,0:T(8,128)S(1)} %bitcast.11), custom_call_target="tpu_custom_call" | custom-call | tf_op jit(solution)/shard_map/pack/pallas_call | solution.py:103
  4.6 0.0 copy-start.1
  4.6 0.0 copy-start.2
  4.6 0.0 copy-start.3
  4.6 0.0 copy-start.4
  4.7 0.0 copy-start.5
  4.7 0.0 copy-start.6
  4.7 0.0 copy-start.7
  4.7 0.0 copy-start.8
  4.7 0.0 copy-start.9
  4.7 65.2 %all_to_all.15 = f32[64,64,128]{2,1,0:T(8,128)S(1)} all-to-all(f32[64,64,128]{2,1,0:T(8,128)S(1)} %bitcast.7), channel_id=1, replica_groups=mesh['tm'=64,'runs'=8] {'tm'}, dimensions={0} | all-to-all | bytes 4194304 | tf_op jit(solution)/shard_map/all_to_all | solution.py:249
  69.9 0.0 copy-done.1
  69.9 0.0 copy-done.2
  69.9 0.0 copy-done.3
  69.9 0.0 copy-done.4
  69.9 0.0 copy-done.5
  70.0 6.6 %dft.1 = f32[64,4,2,8,128]{4,3,2,1,0:T(8,128)S(1)} custom-call(f32[64,2,2,2,8,128]{5,4,3,2,1,0:T(8,128)S(1)} %bitcast.8, f32[512,256]{1,0:T(8,128)S(1)} %copy-done.7, f32[256,256]{1,0:T(8,128)S(1)} %copy-done.9, f32[256,256]{1,0:T(8,128)S(1)} %copy-done.8, bf16[512,512]{1,0:T(8,128)(2,1)S(1)} %copy-done.6, bf16[512,512]{1,0:T(8,128)(2,1)S(1)} %copy-done.5, ...), custom_call_target="tpu_custom_call" | custom-call | tf_op jit(solution)/shard_map/dft/pallas_call | solution.py:140
  76.6 56.5 %all_to_all.16 = f32[64,64,128]{2,1,0:T(8,128)S(1)} all-to-all(f32[64,64,128]{2,1,0:T(8,128)S(1)} %bitcast.9), channel_id=1, replica_groups=mesh['tm'=64,'runs'=8] {'tm'}, dimensions={0} | all-to-all | bytes 4194304 | tf_op jit(solution)/shard_map/all_to_all | solution.py:249
  133.1 1.6 cross.1
  134.7 34.6 %all_to_all.17 = f32[8,2,128,128]{3,2,1,0:T(8,128)S(1)} all-to-all(f32[8,2,128,128]{3,2,1,0:T(8,128)S(1)} %cross.1), channel_id=1, replica_groups=mesh['tm'=64,'runs'=8] {'runs'}, dimensions={0} | all-to-all | bytes 2097152 | tf_op jit(solution)/shard_map/all_to_all | solution.py:249
  169.3 0.0 copy-done.10
  169.3 2.2 %moments.1 = (f32[4,1,2,128,128]{4,3,2,1,0:T(8,128)}, f32[4,1,128,128]{3,2,1,0:T(8,128)}, f32[4,1,2,128,128]{4,3,2,1,0:T(8,128)}) custom-call(s32[16]{0:T(128)S(1)} %copy-done.10, s32[16]{0:T(128)S(1)} %copy-done.11, f32[16,128,128]{2,1,0:T(8,128)S(1)} %bitcast.10), custom_call_target="tpu_custom_call" | custom-call | tf_op jit(solution)/shard_map/moments/pallas_call | solution.py:233
  (7 shorter events, 0.0 us)
Async XLA Ops:
  0.6 1.6 copy-start
  4.6 65.3 %copy-start.1 = (bf16[512,512]{1,0:T(8,128)(2,1)S(1)}, bf16[512,512]{1,0:T(8,128)(2,1)}, u32[]{:S(2)}) copy-start(bf16[512,512]{1,0:T(8,128)(2,1)} %constant.26.clone.el_ref) | copy-start | bytes 1572868
  4.6 65.3 %copy-start.2 = (bf16[512,512]{1,0:T(8,128)(2,1)S(1)}, bf16[512,512]{1,0:T(8,128)(2,1)}, u32[]{:S(2)}) copy-start(bf16[512,512]{1,0:T(8,128)(2,1)} %constant.25.clone.eh_ref) | copy-start | bytes 1572868
  4.6 65.3 %copy-start.3 = (bf16[512,512]{1,0:T(8,128)(2,1)S(1)}, bf16[512,512]{1,0:T(8,128)(2,1)}, u32[]{:S(2)}) copy-start(bf16[512,512]{1,0:T(8,128)(2,1)} %constant.24.clone.sl_ref) | copy-start | bytes 1572868
  4.6 65.3 %copy-start.4 = (bf16[512,512]{1,0:T(8,128)(2,1)S(1)}, bf16[512,512]{1,0:T(8,128)(2,1)}, u32[]{:S(2)}) copy-start(bf16[512,512]{1,0:T(8,128)(2,1)} %constant.23.clone.sh_ref) | copy-start | bytes 1572868
  4.7 65.3 %copy-start.5 = (bf16[512,512]{1,0:T(8,128)(2,1)S(1)}, bf16[512,512]{1,0:T(8,128)(2,1)}, u32[]{:S(2)}) copy-start(bf16[512,512]{1,0:T(8,128)(2,1)} %constant.22.clone.fl_ref) | copy-start | bytes 1572868
  4.7 65.3 %copy-start.6 = (bf16[512,512]{1,0:T(8,128)(2,1)S(1)}, bf16[512,512]{1,0:T(8,128)(2,1)}, u32[]{:S(2)}) copy-start(bf16[512,512]{1,0:T(8,128)(2,1)} %constant.21.clone.fh_ref) | copy-start | bytes 1572868
  4.7 65.3 %copy-start.7 = (f32[512,256]{1,0:T(8,128)S(1)}, f32[512,256]{1,0:T(8,128)}, u32[]{:S(2)}) copy-start(f32[512,256]{1,0:T(8,128)} %constant.18.clone.w_ref) | copy-start | bytes 1572868
  4.7 65.3 %copy-start.8 = (f32[256,256]{1,0:T(8,128)S(1)}, f32[256,256]{1,0:T(8,128)}, u32[]{:S(2)}) copy-start(f32[256,256]{1,0:T(8,128)} %constant.20.clone.s_ref) | copy-start | bytes 786436
  4.7 65.3 %copy-start.9 = (f32[256,256]{1,0:T(8,128)S(1)}, f32[256,256]{1,0:T(8,128)}, u32[]{:S(2)}) copy-start(f32[256,256]{1,0:T(8,128)} %constant.19.clone.c_ref) | copy-start | bytes 786436
  133.1 36.2 %copy-start.10 = (s32[16]{0:T(128)S(1)}, s32[16]{0:T(128)}, u32[]{:S(2)}) copy-start(s32[16]{0:T(128)} %lev_ref.1) | copy-start | bytes 196
  133.1 36.2 %copy-start.11 = (s32[16]{0:T(128)S(1)}, s32[16]{0:T(128)}, u32[]{:S(2)}) copy-start(s32[16]{0:T(128)} %roll_ref.1) | copy-start | bytes 196
where the time goes:
time: 172 us
  blocking collectives  156 us (91%)
  Pallas kernels  12.8 us (7%)
    all_to_all x3, blocking collectives, exchange(): return lax.all_to_all(x, axis, split_axis=0, concat_axis=0, tiled=True)  156 us
    pallas_call x1, Pallas kernels, dft(): pl.pallas_call(dft_kernel, grid=(4,), in_specs=[pl.BlockSpec((64, 1, 1, 2...  6.63 us

commit v1 on v0

v1 whole, which is shorter than its diff:
```python
import functools
import math

import jax
import jax.numpy as jnp
import ml_dtypes
import numpy as np
from jax import lax
from jax.experimental import pallas as pl
from jax.experimental.pallas import tpu as pltpu
from jax.sharding import PartitionSpec as P

CH = 128
BIN = 1024
NC = 4
NQ = 4
TOTAL = 131072
RUNS = 16
NB = 64
T1 = 512
T2 = 256

NT = (((1,), (1,)), ((), ()))
MIB = 1 << 20
STEP = 136


def split_table(table):
    high = table.astype(ml_dtypes.bfloat16)
    low = (table - high.astype(np.float64)).astype(ml_dtypes.bfloat16)
    return high, low


@functools.lru_cache(maxsize=None)
def tables():
    even, odd = np.arange(0, 256, 2), np.arange(1, 256, 2)
    t1 = np.arange(256)

    def trig(k, t, period):
        angle = 2.0 * np.pi * (k[:, None] * t[None, :] % period) / period
        return np.cos(angle), np.sin(angle)

    cos_e, sin_e = trig(even, t1, T1)
    cos_o, sin_o = trig(odd, t1, T1)
    sin_e[0] = -np.cos(np.pi * (t1 % 2))
    first_even = np.concatenate([cos_e, -sin_e], axis=0)
    first_odd = np.concatenate([cos_o, -sin_o], axis=0)
    t2 = np.arange(T2)
    cos_t, sin_t = trig(np.concatenate([even, odd]), t2, TOTAL)
    near = np.arange(128)
    second = np.zeros((2, NB, 2, 2, 2, 128))
    edge = np.zeros((NB, 8, T2))
    for band in range(NB):
        for parity in range(2):
            for m, (k2, sign) in enumerate(
                [(2 * band + parity, 1.0), (254 + parity - 2 * band, -1.0)]
            ):
                a = 2.0 * np.pi * (k2 * near % T2) / T2
                second[parity, band, 0, m, 0] = np.cos(a)
                second[parity, band, 0, m, 1] = np.sin(a)
                second[parity, band, 1, m, 0] = -sign * np.sin(a)
                second[parity, band, 1, m, 1] = sign * np.cos(a)
        for half in range(2):
            for m in range(2):
                a = 2.0 * np.pi * ((2 * (2 * band + m) + half) * t2 % 512) / 512
                edge[band, 4 * half + m] = np.cos(a)
                edge[band, 4 * half + 2 + m] = -np.sin(a)
    t = np.arange(TOTAL).reshape(T1, T2)
    window = 0.5 - 0.5 * np.cos(2.0 * np.pi * t / TOTAL)

    def passes(table):
        high, low = split_table(table)
        return np.concatenate([high, high, low], axis=1)

    return (
        window.astype(np.float32),
        cos_t.astype(np.float32),
        sin_t.astype(np.float32),
        passes(first_even),
        passes(first_odd),
        passes(second[0].reshape(256, 256)),
        passes(second[1].reshape(256, 256)),
        passes(edge.reshape(NB * 8, T2)),
    )


def split(value):
    high = value.astype(jnp.bfloat16)
    low = (value - high.astype(jnp.float32)).astype(jnp.bfloat16)
    return high, low


def dot(a, b):
    return jnp.dot(a, b, preferred_element_type=jnp.float32)


def dot_nt(a, b):
    return lax.dot_general(a, b, NT, preferred_element_type=jnp.float32)


def pack_kernel(x_hbm, o_ref, landed, turned, sems):
    copies = [
        pltpu.make_async_copy(x_hbm.at[r, :, h], landed.at[r, h], sems.at[r, h])
        for r in range(2)
        for h in range(2)
    ]
    for copy in copies:
        copy.start()
    for r in range(2):
        for h in range(2):
            copies[2 * r + h].wait()
            for u in range(8):
                turned[r, h, u * STEP : u * STEP + 128, :] = landed[r, h, u].T
            for ch in range(CH):
                o_ref[ch % 64, ch // 64, r, h] = turned[r, h, pl.ds(ch, 8, stride=STEP), :]


def pack(samples):
    x = samples.reshape(2, 8, 2, 128, CH)
    return pl.pallas_call(
        pack_kernel,
        in_specs=[pl.BlockSpec(memory_space=pltpu.HBM)],
        out_specs=pl.BlockSpec(memory_space=pltpu.VMEM),
        out_shape=jax.ShapeDtypeStruct((64, 2, 2, 2, 8, 128), jnp.float32),
        scratch_shapes=[
            pltpu.VMEM((2, 2, 8, 128, CH), jnp.float32),
            pltpu.VMEM((2, 2, 8 * STEP, 128), jnp.float32),
            pltpu.SemaphoreType.DMA((2, 2)),
        ],
        compiler_params=pltpu.CompilerParams(vmem_limit_bytes=50 * MIB),
        name="pack",
    )(x)


def dft_kernel(
    x_ref, w_ref, c_ref, s_ref, fe_ref, fo_ref, se_ref, so_ref, edge_ref, o_ref, edge_in
):
    edge_in[...] = jnp.zeros_like(edge_in)
    first_row = lax.broadcasted_iota(jnp.int32, (256, T2), 0) == 0
    upper = lax.broadcasted_iota(jnp.int32, (32, 8, 128), 1) < 4

    @pl.loop(0, 4)
    def _(i):
        halves = [x_ref[:, i // 2, i % 2, h].reshape(T1, 128) for h in range(2)]
        x = jnp.concatenate(halves, axis=1) * w_ref[...]
        xh, xl = split(x[:256] + x[256:])
        a_even = dot(fe_ref[...], jnp.concatenate([xh, xl, xh], axis=0))
        xh, xl = split(x[:256] - x[256:])
        a_odd = dot(fo_ref[...], jnp.concatenate([xh, xl, xh], axis=0))
        a_re = jnp.concatenate([a_even[:128], a_odd[:128]], axis=0)
        a_im = jnp.concatenate([a_even[128:], a_odd[128:]], axis=0)
        c, s = c_ref[...], s_ref[...]
        b_re = a_re * c + a_im * s
        b_im = a_im * c - a_re * s
        edge_in[pl.ds(i, 1), :] = b_re[:1]
        edge_in[pl.ds(i + 4, 1), :] = b_im[:1]
        b_re = jnp.where(first_row, 0.0, b_re)
        b_im = jnp.where(first_row, 0.0, b_im)
        plus = jnp.concatenate(
            [b_re[:, :128] + b_re[:, 128:], b_im[:, :128] + b_im[:, 128:]], axis=1
        )
        minus = jnp.concatenate(
            [b_re[:, :128] - b_re[:, 128:], b_im[:, :128] - b_im[:, 128:]], axis=1
        )
        bh, bl = split(plus)
        o_even = dot_nt(se_ref[...], jnp.concatenate([bh, bl, bh], axis=1))
        bh, bl = split(minus)
        o_odd = dot_nt(so_ref[...], jnp.concatenate([bh, bl, bh], axis=1))
        for half in range(2):
            lanes = slice(128 * half, 128 * half + 128)
            e = o_even[:, lanes].reshape(32, 8, 128)
            o = o_odd[:, lanes].reshape(32, 8, 128)
            o_ref[:, 0, i, half] = jnp.where(upper, e, pltpu.roll(o, 4, 1))
            o_ref[:, 1, i, half] = jnp.where(upper, pltpu.roll(e, 4, 1), o)

    eh, el = split(edge_in[...])
    e = dot_nt(edge_ref[...], jnp.concatenate([eh, el, eh], axis=1))
    first_lane = lax.broadcasted_iota(jnp.int32, (512, 128), 1) == 0
    sub = lax.broadcasted_iota(jnp.int32, (512, 128), 0) % 8 < 4
    for i in range(4):
        low = e if i == 0 else pltpu.roll(e, 128 - i, 1)
        value = jnp.where(sub, low, pltpu.roll(e, 124 - i, 1))
        o_ref[:, :, i, 0] += jnp.where(first_lane, value, 0.0).reshape(32, 2, 8, 128)


def dft(x):
    consts = [jnp.asarray(t) for t in tables()]
    vmem = pl.BlockSpec(memory_space=pltpu.VMEM)
    return pl.pallas_call(
        dft_kernel,
        in_specs=[vmem] * (1 + len(consts)),
        out_specs=vmem,
        out_shape=jax.ShapeDtypeStruct((NB // 2, 2, 4, 2, 8, 128), jnp.float32),
        scratch_shapes=[pltpu.VMEM((128, T2), jnp.float32)],
        compiler_params=pltpu.CompilerParams(vmem_limit_bytes=24 * MIB),
        name="dft",
    )(x, *consts)


def cross_kernel(x_ref, o_ref, *, scale):
    row = lax.broadcasted_iota(jnp.int32, (CH, CH), 0)
    col = lax.broadcasted_iota(jnp.int32, (CH, CH), 1)
    for r in range(2):
        parts = []
        for part in range(2):
            for c in range(2):
                cols = [
                    x_ref[pl.ds((c * 2 + r) * 16 + half * 8 + part * 2 + m, 64, stride=64), :]
                    for m in (0, 1, 4, 5)
                    for half in range(2)
                ]
                parts.append(jnp.concatenate(cols, axis=1))
        v = jnp.concatenate(parts, axis=0)
        vh, vl = split(v)
        mixed = dot_nt(vh, vl)
        g = dot_nt(vh, vh) + (mixed + mixed.T)
        real = g[:CH, :CH] + g[CH:, CH:]
        imag = g[CH:, :CH] - g[:CH, CH:]
        packed = jnp.where(row >= col, real, imag) * scale
        for y in range(8):
            o_ref[y, r] = packed


def cross(x):
    scale = 1.0 / (0.375 * BIN * TOTAL)
    return pl.pallas_call(
        functools.partial(cross_kernel, scale=scale),
        in_specs=[pl.BlockSpec(memory_space=pltpu.VMEM)],
        out_specs=pl.BlockSpec(memory_space=pltpu.VMEM),
        out_shape=jax.ShapeDtypeStruct((8, 2, CH, CH), jnp.float32),
        compiler_params=pltpu.CompilerParams(vmem_limit_bytes=24 * MIB),
        name="cross",
    )(x.reshape(64 * 64, 128))


def moments_kernel(
    lev_ref, roll_ref, x_ref, lm_hbm, sp_hbm, rm_hbm, sums, rolls, squares, lm, sp, rm, sems
):
    row = lax.broadcasted_iota(jnp.int32, (CH, CH), 0)
    col = lax.broadcasted_iota(jnp.int32, (CH, CH), 1)
    sums[...] = jnp.zeros_like(sums)
    rolls[...] = jnp.zeros_like(rolls)
    squares[...] = jnp.zeros_like(squares)

    def unpack(m):
        t = m.T
        real = jnp.where(row >= col, m, t)
        imag = jnp.where(row < col, m, jnp.where(row > col, -t, 0.0))
        return real, imag

    def count(ref, level):
        total = jnp.int32(0)
        for r in range(RUNS):
            total += (ref[r] == level).astype(jnp.int32)
        return jnp.maximum(total, 1).astype(jnp.float32)

    for r in range(RUNS):
        rolls[roll_ref[r]] += x_ref[r]
    for q in range(NQ):
        rm[q, 0, 0], rm[q, 0, 1] = unpack(rolls[q] / count(roll_ref, q))
    send_rm = pltpu.make_async_copy(rm, rm_hbm, sems.at[0])
    send_rm.start()
    for r in range(RUNS):
        sums[lev_ref[r]] += x_ref[r]
    for l in range(NC):
        mean = sums[l] / count(lev_ref, l)
        sums[l] = mean
        lm[l, 0, 0], lm[l, 0, 1] = unpack(mean)
    send_lm = pltpu.make_async_copy(lm, lm_hbm, sems.at[1])
    send_lm.start()
    for r in range(RUNS):
        level = lev_ref[r]
        offset = x_ref[r] - sums[level]
        squares[level] += offset * offset
    for l in range(NC):
        s = squares[l]
        sp[l, 0] = BIN * jnp.where(row == col, s, s + s.T)
    send_sp = pltpu.make_async_copy(sp, sp_hbm, sems.at[2])
    send_sp.start()
    send_rm.wait()
    send_lm.wait()
    send_sp.wait()


def moments(cohesion, rolling, x):
    vmem = pl.BlockSpec(memory_space=pltpu.VMEM)
    smem = pl.BlockSpec(memory_space=pltpu.SMEM)
    hbm = pl.BlockSpec(memory_space=pltpu.HBM)
    shapes = [(NC, 1, 2, CH, CH), (NC, 1, CH, CH), (NQ, 1, 2, CH, CH)]
    return pl.pallas_call(
        moments_kernel,
        in_specs=[smem, smem, vmem],
        out_specs=(hbm, hbm, hbm),
        out_shape=tuple(jax.ShapeDtypeStruct(shape, jnp.float32) for shape in shapes),
        scratch_shapes=[pltpu.VMEM((4, CH, CH), jnp.float32)] * 3
        + [pltpu.VMEM(shape, jnp.float32) for shape in shapes]
        + [pltpu.SemaphoreType.DMA((3,))],
        compiler_params=pltpu.CompilerParams(vmem_limit_bytes=16 * MIB),
        name="moments",
    )(cohesion, rolling, x.reshape(RUNS, CH, CH))


def exchange(x, axis):
    return lax.all_to_all(x, axis, split_axis=0, concat_axis=0, tiled=True)


def per_device(samples, cohesion, rolling):
    series = exchange(pack(samples).reshape(64, 64, 128), "tm")
    bins = dft(series.reshape(64, 2, 2, 2, 8, 128))
    band = exchange(bins.reshape(64, 64, 128), "tm")
    gathered = exchange(cross(band), "runs")
    return moments(cohesion, rolling, gathered)


def solution(mesh):
    return jax.shard_map(
        per_device,
        mesh=mesh,
        in_specs=(P("runs", "tm", None), P(), P()),
        out_specs=(
            P(None, "tm", None, None, None),
            P(None, "tm", None, None),
            P(None, "tm", None, None, None),
        ),
        check_vma=False,
    )
```

time: 172 us -> 167 us (0.971)
  Pallas kernels: 12.8 us -> 10.1 us
    pallas_call x3, Pallas kernels: 11.2 us -> 8.48 us  [the longest x1 4.13 us: dft(): pl.pallas_call(dft_kernel, in_specs=[vmem] * (1 + len(consts)), out_specs...]
where the time goes in v1:
time: 167 us
  blocking collectives  156 us (93%)
  Pallas kernels  10.1 us (6%)
    all_to_all x3, blocking collectives, exchange(): return lax.all_to_all(x, axis, split_axis=0, concat_axis=0, tiled=True)  156 us
    pallas_call x1, Pallas kernels, dft(): pl.pallas_call(dft_kernel, in_specs=[vmem] * (1 + len(consts)), out_specs...  4.13 us

profile of v1, /device:TPU:4, one launch (start us, length us, event | category | flops | bytes accessed | tf_op | source)
XLA Modules:
  0.0 167.2 jit_solution(7501543748782004539)
XLA Ops:
  0.6 2.1 %pack.1 = f32[64,2,2,2,8,128]{5,4,3,2,1,0:T(8,128)S(1)} custom-call(f32[2,8,2,128,128]{4,3,2,1,0:T(8,128)} %bitcast.11), custom_call_target="tpu_custom_call" | custom-call | tf_op jit(solution)/shard_map/pack/pallas_call | solution.py:120
  2.8 0.0 copy-start
  2.8 0.0 copy-start.1
  2.8 0.0 copy-start.2
  2.8 0.0 copy-start.3
  2.8 0.0 copy-start.4
  2.8 0.0 copy-start.5
  2.9 0.0 copy-start.6
  2.9 0.0 copy-start.7
  2.9 65.2 %all_to_all.15 = f32[64,64,128]{2,1,0:T(8,128)S(1)} all-to-all(f32[64,64,128]{2,1,0:T(8,128)S(1)} %bitcast.7), channel_id=1, replica_groups=mesh['tm'=64,'runs'=8] {'tm'}, dimensions={0} | all-to-all | bytes 4194304 | tf_op jit(solution)/shard_map/all_to_all | solution.py:304
  68.1 0.0 copy-done
  68.1 0.0 copy-done.1
  68.1 0.0 copy-done.2
  68.1 0.0 copy-done.3
  68.1 0.0 copy-done.4
  68.1 0.0 copy-done.5
  68.1 0.0 copy-done.6
  68.1 0.0 copy-done.7
  68.1 4.1 %dft.1 = f32[32,2,4,2,8,128]{5,4,3,2,1,0:T(8,128)S(1)} custom-call(f32[64,2,2,2,8,128]{5,4,3,2,1,0:T(8,128)S(1)} %bitcast.8, f32[512,256]{1,0:T(8,128)S(1)} %copy-done.1, f32[256,256]{1,0:T(8,128)S(1)} %copy-done.7, f32[256,256]{1,0:T(8,128)S(1)} %copy-done.6, bf16[256,768]{1,0:T(8,128)(2,1)S(1)} %copy-done.5, bf16[256,768]{1,0:T(8,128)(2,1)S(1)} %copy-done.4, ...), custom_call_target="tpu_custom_call" | custom-call | tf_op jit(solution)/shard_map/dft/pallas_call | solution.py:189
  72.3 56.5 %all_to_all.16 = f32[64,64,128]{2,1,0:T(8,128)S(1)} all-to-all(f32[64,64,128]{2,1,0:T(8,128)S(1)} %bitcast.9), channel_id=1, replica_groups=mesh['tm'=64,'runs'=8] {'tm'}, dimensions={0} | all-to-all | bytes 4194304 | tf_op jit(solution)/shard_map/all_to_all | solution.py:304
  128.8 1.6 cross.1
  130.4 34.6 %all_to_all.17 = f32[8,2,128,128]{3,2,1,0:T(8,128)S(1)} all-to-all(f32[8,2,128,128]{3,2,1,0:T(8,128)S(1)} %cross.1), channel_id=1, replica_groups=mesh['tm'=64,'runs'=8] {'runs'}, dimensions={0} | all-to-all | bytes 2097152 | tf_op jit(solution)/shard_map/all_to_all | solution.py:304
  165.0 0.0 copy-done.8
  165.0 2.2 %moments.1 = (f32[4,1,2,128,128]{4,3,2,1,0:T(8,128)}, f32[4,1,128,128]{3,2,1,0:T(8,128)}, f32[4,1,2,128,128]{4,3,2,1,0:T(8,128)}) custom-call(s32[16]{0:T(128)S(1)} %copy-done.8, s32[16]{0:T(128)S(1)} %copy-done.9, f32[16,128,128]{2,1,0:T(8,128)S(1)} %bitcast.10), custom_call_target="tpu_custom_call" | custom-call | tf_op jit(solution)/shard_map/moments/pallas_call | solution.py:290
  (3 shorter events, 0.0 us)
Async XLA Ops:
  2.8 65.3 %copy-start = (bf16[512,768]{1,0:T(8,128)(2,1)S(1)}, bf16[512,768]{1,0:T(8,128)(2,1)}, u32[]{:S(2)}) copy-start(bf16[512,768]{1,0:T(8,128)(2,1)} %constant.23.clone.edge_ref) | copy-start | bytes 2359300
  2.8 65.3 %copy-start.1 = (f32[512,256]{1,0:T(8,128)S(1)}, f32[512,256]{1,0:T(8,128)}, u32[]{:S(2)}) copy-start(f32[512,256]{1,0:T(8,128)} %constant.16.clone.w_ref) | copy-start | bytes 1572868
  2.8 65.3 %copy-start.2 = (bf16[256,768]{1,0:T(8,128)(2,1)S(1)}, bf16[256,768]{1,0:T(8,128)(2,1)}, u32[]{:S(2)}) copy-start(bf16[256,768]{1,0:T(8,128)(2,1)} %constant.22.clone.so_ref) | copy-start | bytes 1179652
  2.8 65.3 %copy-start.3 = (bf16[256,768]{1,0:T(8,128)(2,1)S(1)}, bf16[256,768]{1,0:T(8,128)(2,1)}, u32[]{:S(2)}) copy-start(bf16[256,768]{1,0:T(8,128)(2,1)} %constant.21.clone.se_ref) | copy-start | bytes 1179652
  2.8 65.3 %copy-start.4 = (bf16[256,768]{1,0:T(8,128)(2,1)S(1)}, bf16[256,768]{1,0:T(8,128)(2,1)}, u32[]{:S(2)}) copy-start(bf16[256,768]{1,0:T(8,128)(2,1)} %constant.20.clone.fo_ref) | copy-start | bytes 1179652
  2.8 65.2 %copy-start.5 = (bf16[256,768]{1,0:T(8,128)(2,1)S(1)}, bf16[256,768]{1,0:T(8,128)(2,1)}, u32[]{:S(2)}) copy-start(bf16[256,768]{1,0:T(8,128)(2,1)} %constant.19.clone.fe_ref) | copy-start | bytes 1179652
  2.9 65.2 %copy-start.6 = (f32[256,256]{1,0:T(8,128)S(1)}, f32[256,256]{1,0:T(8,128)}, u32[]{:S(2)}) copy-start(f32[256,256]{1,0:T(8,128)} %constant.18.clone.s_ref) | copy-start | bytes 786436
  2.9 65.2 %copy-start.7 = (f32[256,256]{1,0:T(8,128)S(1)}, f32[256,256]{1,0:T(8,128)}, u32[]{:S(2)}) copy-start(f32[256,256]{1,0:T(8,128)} %constant.17.clone.c_ref) | copy-start | bytes 786436
  128.8 36.2 %copy-start.8 = (s32[16]{0:T(128)S(1)}, s32[16]{0:T(128)}, u32[]{:S(2)}) copy-start(s32[16]{0:T(128)} %lev_ref.1) | copy-start | bytes 196
  128.8 36.2 %copy-start.9 = (s32[16]{0:T(128)S(1)}, s32[16]{0:T(128)}, u32[]{:S(2)}) copy-start(s32[16]{0:T(128)} %roll_ref.1) | copy-start | bytes 196

commit v2 on v1

--- a/solution.py
+++ b/solution.py
@@ -22,6 +22,7 @@
 
 NT = (((1,), (1,)), ((), ()))
 MIB = 1 << 20
+PITCH = 72
 STEP = 136
 
 
@@ -139,7 +140,7 @@
     first_row = lax.broadcasted_iota(jnp.int32, (256, T2), 0) == 0
     upper = lax.broadcasted_iota(jnp.int32, (32, 8, 128), 1) < 4
 
-    @pl.loop(0, 4)
+    @pl.loop(0, 4, unroll=4)
     def _(i):
         halves = [x_ref[:, i // 2, i % 2, h].reshape(T1, 128) for h in range(2)]
         x = jnp.concatenate(halves, axis=1) * w_ref[...]
@@ -197,15 +198,17 @@
     )(x, *consts)
 
 
-def cross_kernel(x_ref, o_ref, *, scale):
+def cross_kernel(x_ref, o_ref, rows, *, scale):
     row = lax.broadcasted_iota(jnp.int32, (CH, CH), 0)
     col = lax.broadcasted_iota(jnp.int32, (CH, CH), 1)
+    for q in range(64):
+        rows[q * PITCH : q * PITCH + 64, :] = x_ref[q * 64 : q * 64 + 64, :]
     for r in range(2):
         parts = []
         for part in range(2):
             for c in range(2):
                 cols = [
-                    x_ref[pl.ds((c * 2 + r) * 16 + half * 8 + part * 2 + m, 64, stride=64), :]
+                    rows[pl.ds((c * 2 + r) * 16 + half * 8 + part * 2 + m, 64, stride=PITCH), :]
                     for m in (0, 1, 4, 5)
                     for half in range(2)
                 ]
@@ -228,6 +231,7 @@
         in_specs=[pl.BlockSpec(memory_space=pltpu.VMEM)],
         out_specs=pl.BlockSpec(memory_space=pltpu.VMEM),
         out_shape=jax.ShapeDtypeStruct((8, 2, CH, CH), jnp.float32),
+        scratch_shapes=[pltpu.VMEM((64 * PITCH, 128), jnp.float32)],
         compiler_params=pltpu.CompilerParams(vmem_limit_bytes=24 * MIB),
         name="cross",
     )(x.reshape(64 * 64, 128))

time: 167 us -> 166 us (level)
  no operation moved by 1% of the time
where the time goes in v2:
time: 166 us
  blocking collectives  156 us (94%)
  Pallas kernels  8.9 us (5%)
    all_to_all x3, blocking collectives, exchange(): return lax.all_to_all(x, axis, split_axis=0, concat_axis=0, tiled=True)  156 us
    pallas_call x1, Pallas kernels, dft(): pl.pallas_call(dft_kernel, in_specs=[vmem] * (1 + len(consts)), out_specs...  3.5 us

profile of v2, /device:TPU:4, one launch (start us, length us, event | category | flops | bytes accessed | tf_op | source)
XLA Modules:
  0.0 166.0 jit_solution(9492772643799651471)
XLA Ops:
  0.6 2.1 %pack.1 = f32[64,2,2,2,8,128]{5,4,3,2,1,0:T(8,128)S(1)} custom-call(f32[2,8,2,128,128]{4,3,2,1,0:T(8,128)} %bitcast.11), custom_call_target="tpu_custom_call" | custom-call | tf_op jit(solution)/shard_map/pack/pallas_call | solution.py:121
  2.8 0.0 copy-start
  2.8 0.0 copy-start.1
  2.8 0.0 copy-start.2
  2.8 0.0 copy-start.3
  2.8 0.0 copy-start.4
  2.8 0.0 copy-start.5
  2.9 0.0 copy-start.6
  2.9 0.0 copy-start.7
  2.9 65.2 %all_to_all.15 = f32[64,64,128]{2,1,0:T(8,128)S(1)} all-to-all(f32[64,64,128]{2,1,0:T(8,128)S(1)} %bitcast.7), channel_id=1, replica_groups=mesh['tm'=64,'runs'=8] {'tm'}, dimensions={0} | all-to-all | bytes 4194304 | tf_op jit(solution)/shard_map/all_to_all | solution.py:308
  68.1 0.0 copy-done
  68.1 0.0 copy-done.1
  68.1 0.0 copy-done.2
  68.1 0.0 copy-done.3
  68.1 0.0 copy-done.4
  68.1 0.0 copy-done.5
  68.1 0.0 copy-done.6
  68.1 0.0 copy-done.7
  68.1 3.5 %dft.1 = f32[32,2,4,2,8,128]{5,4,3,2,1,0:T(8,128)S(1)} custom-call(f32[64,2,2,2,8,128]{5,4,3,2,1,0:T(8,128)S(1)} %bitcast.8, f32[512,256]{1,0:T(8,128)S(1)} %copy-done.1, f32[256,256]{1,0:T(8,128)S(1)} %copy-done.7, f32[256,256]{1,0:T(8,128)S(1)} %copy-done.6, bf16[256,768]{1,0:T(8,128)(2,1)S(1)} %copy-done.5, bf16[256,768]{1,0:T(8,128)(2,1)S(1)} %copy-done.4, ...), custom_call_target="tpu_custom_call" | custom-call | tf_op jit(solution)/shard_map/dft/pallas_call | solution.py:190
  71.6 56.5 %all_to_all.16 = f32[64,64,128]{2,1,0:T(8,128)S(1)} all-to-all(f32[64,64,128]{2,1,0:T(8,128)S(1)} %bitcast.9), channel_id=1, replica_groups=mesh['tm'=64,'runs'=8] {'tm'}, dimensions={0} | all-to-all | bytes 4194304 | tf_op jit(solution)/shard_map/all_to_all | solution.py:308
  128.1 1.1 cross.1
  129.2 34.6 %all_to_all.17 = f32[8,2,128,128]{3,2,1,0:T(8,128)S(1)} all-to-all(f32[8,2,128,128]{3,2,1,0:T(8,128)S(1)} %cross.1), channel_id=1, replica_groups=mesh['tm'=64,'runs'=8] {'runs'}, dimensions={0} | all-to-all | bytes 2097152 | tf_op jit(solution)/shard_map/all_to_all | solution.py:308
  163.8 0.0 copy-done.9
  163.8 2.2 %moments.1 = (f32[4,1,2,128,128]{4,3,2,1,0:T(8,128)}, f32[4,1,128,128]{3,2,1,0:T(8,128)}, f32[4,1,2,128,128]{4,3,2,1,0:T(8,128)}) custom-call(s32[16]{0:T(128)S(1)} %copy-done.8, s32[16]{0:T(128)S(1)} %copy-done.9, f32[16,128,128]{2,1,0:T(8,128)S(1)} %bitcast.10), custom_call_target="tpu_custom_call" | custom-call | tf_op jit(solution)/shard_map/moments/pallas_call | solution.py:294
  (3 shorter events, 0.0 us)
Async XLA Ops:
  2.8 65.3 %copy-start = (bf16[512,768]{1,0:T(8,128)(2,1)S(1)}, bf16[512,768]{1,0:T(8,128)(2,1)}, u32[]{:S(2)}) copy-start(bf16[512,768]{1,0:T(8,128)(2,1)} %constant.23.clone.edge_ref) | copy-start | bytes 2359300
  2.8 65.3 %copy-start.1 = (f32[512,256]{1,0:T(8,128)S(1)}, f32[512,256]{1,0:T(8,128)}, u32[]{:S(2)}) copy-start(f32[512,256]{1,0:T(8,128)} %constant.16.clone.w_ref) | copy-start | bytes 1572868
  2.8 65.3 %copy-start.2 = (bf16[256,768]{1,0:T(8,128)(2,1)S(1)}, bf16[256,768]{1,0:T(8,128)(2,1)}, u32[]{:S(2)}) copy-start(bf16[256,768]{1,0:T(8,128)(2,1)} %constant.22.clone.so_ref) | copy-start | bytes 1179652
  2.8 65.3 %copy-start.3 = (bf16[256,768]{1,0:T(8,128)(2,1)S(1)}, bf16[256,768]{1,0:T(8,128)(2,1)}, u32[]{:S(2)}) copy-start(bf16[256,768]{1,0:T(8,128)(2,1)} %constant.21.clone.se_ref) | copy-start | bytes 1179652
  2.8 65.3 %copy-start.4 = (bf16[256,768]{1,0:T(8,128)(2,1)S(1)}, bf16[256,768]{1,0:T(8,128)(2,1)}, u32[]{:S(2)}) copy-start(bf16[256,768]{1,0:T(8,128)(2,1)} %constant.20.clone.fo_ref) | copy-start | bytes 1179652
  2.8 65.2 %copy-start.5 = (bf16[256,768]{1,0:T(8,128)(2,1)S(1)}, bf16[256,768]{1,0:T(8,128)(2,1)}, u32[]{:S(2)}) copy-start(bf16[256,768]{1,0:T(8,128)(2,1)} %constant.19.clone.fe_ref) | copy-start | bytes 1179652
  2.9 65.2 %copy-start.6 = (f32[256,256]{1,0:T(8,128)S(1)}, f32[256,256]{1,0:T(8,128)}, u32[]{:S(2)}) copy-start(f32[256,256]{1,0:T(8,128)} %constant.18.clone.s_ref) | copy-start | bytes 786436
  2.9 65.2 %copy-start.7 = (f32[256,256]{1,0:T(8,128)S(1)}, f32[256,256]{1,0:T(8,128)}, u32[]{:S(2)}) copy-start(f32[256,256]{1,0:T(8,128)} %constant.17.clone.c_ref) | copy-start | bytes 786436
  128.1 35.7 %copy-start.8 = (s32[16]{0:T(128)S(1)}, s32[16]{0:T(128)}, u32[]{:S(2)}) copy-start(s32[16]{0:T(128)} %lev_ref.1) | copy-start | bytes 196
  128.1 35.7 %copy-start.9 = (s32[16]{0:T(128)S(1)}, s32[16]{0:T(128)}, u32[]{:S(2)}) copy-start(s32[16]{0:T(128)} %roll_ref.1) | copy-start | bytes 196

commit v3 on v2

--- a/solution.py
+++ b/solution.py
@@ -134,14 +134,13 @@
 
 
 def dft_kernel(
-    x_ref, w_ref, c_ref, s_ref, fe_ref, fo_ref, se_ref, so_ref, edge_ref, o_ref, edge_in
+    x_ref, w_ref, c_ref, s_ref, fe_ref, fo_ref, se_ref, so_ref, edge_ref, o_ref, edge_in, middle
 ):
     edge_in[...] = jnp.zeros_like(edge_in)
     first_row = lax.broadcasted_iota(jnp.int32, (256, T2), 0) == 0
     upper = lax.broadcasted_iota(jnp.int32, (32, 8, 128), 1) < 4
 
-    @pl.loop(0, 4, unroll=4)
-    def _(i):
+    for i in range(4):
         halves = [x_ref[:, i // 2, i % 2, h].reshape(T1, 128) for h in range(2)]
         x = jnp.concatenate(halves, axis=1) * w_ref[...]
         xh, xl = split(x[:256] + x[256:])
@@ -153,8 +152,8 @@
         c, s = c_ref[...], s_ref[...]
         b_re = a_re * c + a_im * s
         b_im = a_im * c - a_re * s
-        edge_in[pl.ds(i, 1), :] = b_re[:1]
-        edge_in[pl.ds(i + 4, 1), :] = b_im[:1]
+        edge_in[i : i + 1, :] = b_re[:1]
+        edge_in[i + 4 : i + 5, :] = b_im[:1]
         b_re = jnp.where(first_row, 0.0, b_re)
         b_im = jnp.where(first_row, 0.0, b_im)
         plus = jnp.concatenate(
@@ -163,25 +162,30 @@
         minus = jnp.concatenate(
             [b_re[:, :128] - b_re[:, 128:], b_im[:, :128] - b_im[:, 128:]], axis=1
         )
-        bh, bl = split(plus)
+        middle[i, 0, 0], middle[i, 0, 1] = split(plus)
+        middle[i, 1, 0], middle[i, 1, 1] = split(minus)
+
+    eh, el = split(edge_in[...])
+    edge = dot_nt(edge_ref[...], jnp.concatenate([eh, el, eh], axis=1))
+    first_lane = lax.broadcasted_iota(jnp.int32, (512, 128), 1) == 0
+    sub = lax.broadcasted_iota(jnp.int32, (512, 128), 0) % 8 < 4
+
+    for i in range(4):
+        bh, bl = middle[i, 0, 0], middle[i, 0, 1]
         o_even = dot_nt(se_ref[...], jnp.concatenate([bh, bl, bh], axis=1))
-        bh, bl = split(minus)
+        bh, bl = middle[i, 1, 0], middle[i, 1, 1]
         o_odd = dot_nt(so_ref[...], jnp.concatenate([bh, bl, bh], axis=1))
+        low = edge if i == 0 else pltpu.roll(edge, 128 - i, 1)
+        extra = jnp.where(sub, low, pltpu.roll(edge, 124 - i, 1))
+        extra = jnp.where(first_lane, extra, 0.0).reshape(32, 2, 8, 128)
         for half in range(2):
             lanes = slice(128 * half, 128 * half + 128)
             e = o_even[:, lanes].reshape(32, 8, 128)
             o = o_odd[:, lanes].reshape(32, 8, 128)
-            o_ref[:, 0, i, half] = jnp.where(upper, e, pltpu.roll(o, 4, 1))
-            o_ref[:, 1, i, half] = jnp.where(upper, pltpu.roll(e, 4, 1), o)
-
-    eh, el = split(edge_in[...])
-    e = dot_nt(edge_ref[...], jnp.concatenate([eh, el, eh], axis=1))
-    first_lane = lax.broadcasted_iota(jnp.int32, (512, 128), 1) == 0
-    sub = lax.broadcasted_iota(jnp.int32, (512, 128), 0) % 8 < 4
-    for i in range(4):
-        low = e if i == 0 else pltpu.roll(e, 128 - i, 1)
-        value = jnp.where(sub, low, pltpu.roll(e, 124 - i, 1))
-        o_ref[:, :, i, 0] += jnp.where(first_lane, value, 0.0).reshape(32, 2, 8, 128)
+            first = jnp.where(upper, e, pltpu.roll(o, 4, 1))
+            second = jnp.where(upper, pltpu.roll(e, 4, 1), o)
+            o_ref[:, 0, i, half] = first + extra[:, 0] if half == 0 else first
+            o_ref[:, 1, i, half] = second + extra[:, 1] if half == 0 else second
 
 
 def dft(x):
@@ -192,7 +196,10 @@
         in_specs=[vmem] * (1 + len(consts)),
         out_specs=vmem,
         out_shape=jax.ShapeDtypeStruct((NB // 2, 2, 4, 2, 8, 128), jnp.float32),
-        scratch_shapes=[pltpu.VMEM((128, T2), jnp.float32)],
+        scratch_shapes=[
+            pltpu.VMEM((128, T2), jnp.float32),
+            pltpu.VMEM((4, 2, 2, 256, 256), jnp.bfloat16),
+        ],
         compiler_params=pltpu.CompilerParams(vmem_limit_bytes=24 * MIB),
         name="dft",
     )(x, *consts)
@@ -238,10 +245,13 @@
 
 
 def moments_kernel(
-    lev_ref, roll_ref, x_ref, lm_hbm, sp_hbm, rm_hbm, sums, rolls, squares, lm, sp, rm, sems
+    lev_vec, roll_vec, x_ref, lm_hbm, sp_hbm, rm_hbm, sums, rolls, squares, lm, sp, rm, sems
 ):
     row = lax.broadcasted_iota(jnp.int32, (CH, CH), 0)
     col = lax.broadcasted_iota(jnp.int32, (CH, CH), 1)
+    levels, turns = lev_vec[...], roll_vec[...]
+    lev_ref = [levels[0, r] for r in range(RUNS)]
+    roll_ref = [turns[0, r] for r in range(RUNS)]
     sums[...] = jnp.zeros_like(sums)
     rolls[...] = jnp.zeros_like(rolls)
     squares[...] = jnp.zeros_like(squares)
@@ -258,20 +268,25 @@
             total += (ref[r] == level).astype(jnp.int32)
         return jnp.maximum(total, 1).astype(jnp.float32)
 
+    sends = []
+
+    def send(source, target, kind, level):
+        copy = pltpu.make_async_copy(source.at[level], target.at[level], sems.at[kind, level])
+        copy.start()
+        sends.append(copy)
+
     for r in range(RUNS):
         rolls[roll_ref[r]] += x_ref[r]
     for q in range(NQ):
         rm[q, 0, 0], rm[q, 0, 1] = unpack(rolls[q] / count(roll_ref, q))
-    send_rm = pltpu.make_async_copy(rm, rm_hbm, sems.at[0])
-    send_rm.start()
+        send(rm, rm_hbm, 0, q)
     for r in range(RUNS):
         sums[lev_ref[r]] += x_ref[r]
     for l in range(NC):
         mean = sums[l] / count(lev_ref, l)
         sums[l] = mean
         lm[l, 0, 0], lm[l, 0, 1] = unpack(mean)
-    send_lm = pltpu.make_async_copy(lm, lm_hbm, sems.at[1])
-    send_lm.start()
+        send(lm, lm_hbm, 1, l)
     for r in range(RUNS):
         level = lev_ref[r]
         offset = x_ref[r] - sums[level]
@@ -279,11 +294,9 @@
     for l in range(NC):
         s = squares[l]
         sp[l, 0] = BIN * jnp.where(row == col, s, s + s.T)
-    send_sp = pltpu.make_async_copy(sp, sp_hbm, sems.at[2])
-    send_sp.start()
-    send_rm.wait()
-    send_lm.wait()
-    send_sp.wait()
+        send(sp, sp_hbm, 2, l)
+    for copy in sends:
+        copy.wait()
 
 
 def moments(cohesion, rolling, x):
@@ -293,15 +306,15 @@
     shapes = [(NC, 1, 2, CH, CH), (NC, 1, CH, CH), (NQ, 1, 2, CH, CH)]
     return pl.pallas_call(
         moments_kernel,
-        in_specs=[smem, smem, vmem],
+        in_specs=[vmem, vmem, vmem],
         out_specs=(hbm, hbm, hbm),
         out_shape=tuple(jax.ShapeDtypeStruct(shape, jnp.float32) for shape in shapes),
         scratch_shapes=[pltpu.VMEM((4, CH, CH), jnp.float32)] * 3
         + [pltpu.VMEM(shape, jnp.float32) for shape in shapes]
-        + [pltpu.SemaphoreType.DMA((3,))],
+        + [pltpu.SemaphoreType.DMA((3, 4))],
         compiler_params=pltpu.CompilerParams(vmem_limit_bytes=16 * MIB),
         name="moments",
-    )(cohesion, rolling, x.reshape(RUNS, CH, CH))
+    )(cohesion.reshape(1, RUNS), rolling.reshape(1, RUNS), x.reshape(RUNS, CH, CH))
 
 
 def exchange(x, axis):

time: 166 us -> 165 us (level)
  no operation moved by 1% of the time
where the time goes in v3:
time: 165 us
  blocking collectives  156 us (95%)
  Pallas kernels  7.62 us (5%)
    all_to_all x3, blocking collectives, exchange(): return lax.all_to_all(x, axis, split_axis=0, concat_axis=0, tiled=True)  156 us

profile of v3, /device:TPU:4, one launch (start us, length us, event | category | flops | bytes accessed | tf_op | source)
XLA Modules:
  0.0 164.7 jit_solution(13687047228214693897)
XLA Ops:
  0.6 2.1 %pack.1 = f32[64,2,2,2,8,128]{5,4,3,2,1,0:T(8,128)S(1)} custom-call(f32[2,8,2,128,128]{4,3,2,1,0:T(8,128)} %bitcast.15), custom_call_target="tpu_custom_call" | custom-call | tf_op jit(solution)/shard_map/pack/pallas_call | solution.py:121
  2.8 0.0 copy-start
  2.8 0.0 copy-start.1
  2.8 0.0 copy-start.2
  2.8 0.0 copy-start.3
  2.8 0.0 copy-start.4
  2.8 0.0 copy-start.5
  2.9 0.0 copy-start.6
  2.9 0.0 copy-start.7
  2.9 65.2 %all_to_all.15 = f32[64,64,128]{2,1,0:T(8,128)S(1)} all-to-all(f32[64,64,128]{2,1,0:T(8,128)S(1)} %bitcast.9), channel_id=1, replica_groups=mesh['tm'=64,'runs'=8] {'tm'}, dimensions={0} | all-to-all | bytes 4194304 | tf_op jit(solution)/shard_map/all_to_all | solution.py:321
  68.1 0.0 copy-done
  68.1 0.0 copy-done.1
  68.1 0.0 copy-done.2
  68.1 0.0 copy-done.3
  68.1 0.0 copy-done.4
  68.1 0.0 copy-done.5
  68.1 0.0 copy-done.6
  68.1 0.0 copy-done.7
  68.1 2.6 %dft.1 = f32[32,2,4,2,8,128]{5,4,3,2,1,0:T(8,128)S(1)} custom-call(f32[64,2,2,2,8,128]{5,4,3,2,1,0:T(8,128)S(1)} %bitcast.10, f32[512,256]{1,0:T(8,128)S(1)} %copy-done.1, f32[256,256]{1,0:T(8,128)S(1)} %copy-done.7, f32[256,256]{1,0:T(8,128)S(1)} %copy-done.6, bf16[256,768]{1,0:T(8,128)(2,1)S(1)} %copy-done.5, bf16[256,768]{1,0:T(8,128)(2,1)S(1)} %copy-done.4, ...), custom_call_target="tpu_custom_call" | custom-call | tf_op jit(solution)/shard_map/dft/pallas_call | solution.py:194
  70.7 56.5 %all_to_all.16 = f32[64,64,128]{2,1,0:T(8,128)S(1)} all-to-all(f32[64,64,128]{2,1,0:T(8,128)S(1)} %bitcast.11), channel_id=1, replica_groups=mesh['tm'=64,'runs'=8] {'tm'}, dimensions={0} | all-to-all | bytes 4194304 | tf_op jit(solution)/shard_map/all_to_all | solution.py:321
  127.2 1.1 cross.1
  128.3 34.6 %all_to_all.17 = f32[8,2,128,128]{3,2,1,0:T(8,128)S(1)} all-to-all(f32[8,2,128,128]{3,2,1,0:T(8,128)S(1)} %cross.1), channel_id=1, replica_groups=mesh['tm'=64,'runs'=8] {'runs'}, dimensions={0} | all-to-all | bytes 2097152 | tf_op jit(solution)/shard_map/all_to_all | solution.py:321
  162.9 0.0 copy-done.8
  162.9 1.8 %moments.1 = (f32[4,1,2,128,128]{4,3,2,1,0:T(8,128)}, f32[4,1,128,128]{3,2,1,0:T(8,128)}, f32[4,1,2,128,128]{4,3,2,1,0:T(8,128)}) custom-call(s32[1,16]{1,0:T(1,128)S(1)} %bitcast.13, s32[1,16]{1,0:T(1,128)S(1)} %bitcast.14, f32[16,128,128]{2,1,0:T(8,128)S(1)} %bitcast.12), custom_call_target="tpu_custom_call" | custom-call | tf_op jit(solution)/shard_map/moments/pallas_call | solution.py:307
  (3 shorter events, 0.0 us)
Async XLA Ops:
  2.8 65.3 %copy-start = (bf16[512,768]{1,0:T(8,128)(2,1)S(1)}, bf16[512,768]{1,0:T(8,128)(2,1)}, u32[]{:S(2)}) copy-start(bf16[512,768]{1,0:T(8,128)(2,1)} %constant.23.clone.edge_ref) | copy-start | bytes 2359300
  2.8 65.3 %copy-start.1 = (f32[512,256]{1,0:T(8,128)S(1)}, f32[512,256]{1,0:T(8,128)}, u32[]{:S(2)}) copy-start(f32[512,256]{1,0:T(8,128)} %constant.16.clone.w_ref) | copy-start | bytes 1572868
  2.8 65.3 %copy-start.2 = (bf16[256,768]{1,0:T(8,128)(2,1)S(1)}, bf16[256,768]{1,0:T(8,128)(2,1)}, u32[]{:S(2)}) copy-start(bf16[256,768]{1,0:T(8,128)(2,1)} %constant.22.clone.so_ref) | copy-start | bytes 1179652
  2.8 65.3 %copy-start.3 = (bf16[256,768]{1,0:T(8,128)(2,1)S(1)}, bf16[256,768]{1,0:T(8,128)(2,1)}, u32[]{:S(2)}) copy-start(bf16[256,768]{1,0:T(8,128)(2,1)} %constant.21.clone.se_ref) | copy-start | bytes 1179652
  2.8 65.3 %copy-start.4 = (bf16[256,768]{1,0:T(8,128)(2,1)S(1)}, bf16[256,768]{1,0:T(8,128)(2,1)}, u32[]{:S(2)}) copy-start(bf16[256,768]{1,0:T(8,128)(2,1)} %constant.20.clone.fo_ref) | copy-start | bytes 1179652
  2.8 65.2 %copy-start.5 = (bf16[256,768]{1,0:T(8,128)(2,1)S(1)}, bf16[256,768]{1,0:T(8,128)(2,1)}, u32[]{:S(2)}) copy-start(bf16[256,768]{1,0:T(8,128)(2,1)} %constant.19.clone.fe_ref) | copy-start | bytes 1179652
  2.9 65.2 %copy-start.6 = (f32[256,256]{1,0:T(8,128)S(1)}, f32[256,256]{1,0:T(8,128)}, u32[]{:S(2)}) copy-start(f32[256,256]{1,0:T(8,128)} %constant.18.clone.s_ref) | copy-start | bytes 786436
  2.9 65.2 %copy-start.7 = (f32[256,256]{1,0:T(8,128)S(1)}, f32[256,256]{1,0:T(8,128)}, u32[]{:S(2)}) copy-start(f32[256,256]{1,0:T(8,128)} %constant.17.clone.c_ref) | copy-start | bytes 786436
  127.2 35.7 %copy-start.8 = (s32[16]{0:T(128)S(1)}, s32[16]{0:T(128)}, u32[]{:S(2)}) copy-start(s32[16]{0:T(128)} %param.12) | copy-start | bytes 196
  127.2 35.7 %copy-start.9 = (s32[16]{0:T(128)S(1)}, s32[16]{0:T(128)}, u32[]{:S(2)}) copy-start(s32[16]{0:T(128)} %param.13) | copy-start | bytes 196

commit v4 on v3

--- a/solution.py
+++ b/solution.py
@@ -125,7 +125,7 @@
         out_shape=jax.ShapeDtypeStruct((64, 2, 2, 2, 8, 128), jnp.float32),
         scratch_shapes=[
             pltpu.VMEM((2, 2, 8, 128, CH), jnp.float32),
-            pltpu.VMEM((2, 2, 8 * STEP, 128), jnp.float32),
+            pltpu.VMEM((2, 2, 9 * STEP, 128), jnp.float32),
             pltpu.SemaphoreType.DMA((2, 2)),
         ],
         compiler_params=pltpu.CompilerParams(vmem_limit_bytes=50 * MIB),
@@ -238,7 +238,7 @@
         in_specs=[pl.BlockSpec(memory_space=pltpu.VMEM)],
         out_specs=pl.BlockSpec(memory_space=pltpu.VMEM),
         out_shape=jax.ShapeDtypeStruct((8, 2, CH, CH), jnp.float32),
-        scratch_shapes=[pltpu.VMEM((64 * PITCH, 128), jnp.float32)],
+        scratch_shapes=[pltpu.VMEM((65 * PITCH, 128), jnp.float32)],
         compiler_params=pltpu.CompilerParams(vmem_limit_bytes=24 * MIB),
         name="cross",
     )(x.reshape(64 * 64, 128))

time: 165 us -> 165 us (level)
  no operation moved by 1% of the time
where the time goes in v4:
time: 165 us
  blocking collectives  156 us (95%)
  Pallas kernels  7.61 us (5%)
    all_to_all x3, blocking collectives, exchange(): return lax.all_to_all(x, axis, split_axis=0, concat_axis=0, tiled=True)  156 us

profile of v4, /device:TPU:4, one launch (start us, length us, event | category | flops | bytes accessed | tf_op | source)
XLA Modules:
  0.0 164.7 jit_solution(17695742347484880532)
XLA Ops:
  0.6 2.1 %pack.1 = f32[64,2,2,2,8,128]{5,4,3,2,1,0:T(8,128)S(1)} custom-call(f32[2,8,2,128,128]{4,3,2,1,0:T(8,128)} %bitcast.15), custom_call_target="tpu_custom_call" | custom-call | tf_op jit(solution)/shard_map/pack/pallas_call | solution.py:121
  2.8 0.0 copy-start
  2.8 0.0 copy-start.1
  2.8 0.0 copy-start.2
  2.8 0.0 copy-start.3
  2.8 0.0 copy-start.4
  2.8 0.0 copy-start.5
  2.9 0.0 copy-start.6
  2.9 0.0 copy-start.7
  2.9 65.2 %all_to_all.15 = f32[64,64,128]{2,1,0:T(8,128)S(1)} all-to-all(f32[64,64,128]{2,1,0:T(8,128)S(1)} %bitcast.9), channel_id=1, replica_groups=mesh['tm'=64,'runs'=8] {'tm'}, dimensions={0} | all-to-all | bytes 4194304 | tf_op jit(solution)/shard_map/all_to_all | solution.py:321
  68.1 0.0 copy-done
  68.1 0.0 copy-done.1
  68.1 0.0 copy-done.2
  68.1 0.0 copy-done.3
  68.1 0.0 copy-done.4
  68.1 0.0 copy-done.5
  68.1 0.0 copy-done.6
  68.1 0.0 copy-done.7
  68.1 2.6 %dft.1 = f32[32,2,4,2,8,128]{5,4,3,2,1,0:T(8,128)S(1)} custom-call(f32[64,2,2,2,8,128]{5,4,3,2,1,0:T(8,128)S(1)} %bitcast.10, f32[512,256]{1,0:T(8,128)S(1)} %copy-done.1, f32[256,256]{1,0:T(8,128)S(1)} %copy-done.7, f32[256,256]{1,0:T(8,128)S(1)} %copy-done.6, bf16[256,768]{1,0:T(8,128)(2,1)S(1)} %copy-done.5, bf16[256,768]{1,0:T(8,128)(2,1)S(1)} %copy-done.4, ...), custom_call_target="tpu_custom_call" | custom-call | tf_op jit(solution)/shard_map/dft/pallas_call | solution.py:194
  70.7 56.5 %all_to_all.16 = f32[64,64,128]{2,1,0:T(8,128)S(1)} all-to-all(f32[64,64,128]{2,1,0:T(8,128)S(1)} %bitcast.11), channel_id=1, replica_groups=mesh['tm'=64,'runs'=8] {'tm'}, dimensions={0} | all-to-all | bytes 4194304 | tf_op jit(solution)/shard_map/all_to_all | solution.py:321
  127.2 1.0 cross.1
  128.3 34.6 %all_to_all.17 = f32[8,2,128,128]{3,2,1,0:T(8,128)S(1)} all-to-all(f32[8,2,128,128]{3,2,1,0:T(8,128)S(1)} %cross.1), channel_id=1, replica_groups=mesh['tm'=64,'runs'=8] {'runs'}, dimensions={0} | all-to-all | bytes 2097152 | tf_op jit(solution)/shard_map/all_to_all | solution.py:321
  162.9 0.0 copy-done.8
  162.9 1.8 %moments.1 = (f32[4,1,2,128,128]{4,3,2,1,0:T(8,128)}, f32[4,1,128,128]{3,2,1,0:T(8,128)}, f32[4,1,2,128,128]{4,3,2,1,0:T(8,128)}) custom-call(s32[1,16]{1,0:T(1,128)S(1)} %bitcast.13, s32[1,16]{1,0:T(1,128)S(1)} %bitcast.14, f32[16,128,128]{2,1,0:T(8,128)S(1)} %bitcast.12), custom_call_target="tpu_custom_call" | custom-call | tf_op jit(solution)/shard_map/moments/pallas_call | solution.py:307
  (3 shorter events, 0.0 us)
Async XLA Ops:
  2.8 65.3 %copy-start = (bf16[512,768]{1,0:T(8,128)(2,1)S(1)}, bf16[512,768]{1,0:T(8,128)(2,1)}, u32[]{:S(2)}) copy-start(bf16[512,768]{1,0:T(8,128)(2,1)} %constant.23.clone.edge_ref) | copy-start | bytes 2359300
  2.8 65.3 %copy-start.1 = (f32[512,256]{1,0:T(8,128)S(1)}, f32[512,256]{1,0:T(8,128)}, u32[]{:S(2)}) copy-start(f32[512,256]{1,0:T(8,128)} %constant.16.clone.w_ref) | copy-start | bytes 1572868
  2.8 65.3 %copy-start.2 = (bf16[256,768]{1,0:T(8,128)(2,1)S(1)}, bf16[256,768]{1,0:T(8,128)(2,1)}, u32[]{:S(2)}) copy-start(bf16[256,768]{1,0:T(8,128)(2,1)} %constant.22.clone.so_ref) | copy-start | bytes 1179652
  2.8 65.3 %copy-start.3 = (bf16[256,768]{1,0:T(8,128)(2,1)S(1)}, bf16[256,768]{1,0:T(8,128)(2,1)}, u32[]{:S(2)}) copy-start(bf16[256,768]{1,0:T(8,128)(2,1)} %constant.21.clone.se_ref) | copy-start | bytes 1179652
  2.8 65.3 %copy-start.4 = (bf16[256,768]{1,0:T(8,128)(2,1)S(1)}, bf16[256,768]{1,0:T(8,128)(2,1)}, u32[]{:S(2)}) copy-start(bf16[256,768]{1,0:T(8,128)(2,1)} %constant.20.clone.fo_ref) | copy-start | bytes 1179652
  2.8 65.2 %copy-start.5 = (bf16[256,768]{1,0:T(8,128)(2,1)S(1)}, bf16[256,768]{1,0:T(8,128)(2,1)}, u32[]{:S(2)}) copy-start(bf16[256,768]{1,0:T(8,128)(2,1)} %constant.19.clone.fe_ref) | copy-start | bytes 1179652
  2.9 65.2 %copy-start.6 = (f32[256,256]{1,0:T(8,128)S(1)}, f32[256,256]{1,0:T(8,128)}, u32[]{:S(2)}) copy-start(f32[256,256]{1,0:T(8,128)} %constant.18.clone.s_ref) | copy-start | bytes 786436
  2.9 65.2 %copy-start.7 = (f32[256,256]{1,0:T(8,128)S(1)}, f32[256,256]{1,0:T(8,128)}, u32[]{:S(2)}) copy-start(f32[256,256]{1,0:T(8,128)} %constant.17.clone.c_ref) | copy-start | bytes 786436
  127.2 35.7 %copy-start.8 = (s32[16]{0:T(128)S(1)}, s32[16]{0:T(128)}, u32[]{:S(2)}) copy-start(s32[16]{0:T(128)} %param.12) | copy-start | bytes 196
  127.2 35.7 %copy-start.9 = (s32[16]{0:T(128)S(1)}, s32[16]{0:T(128)}, u32[]{:S(2)}) copy-start(s32[16]{0:T(128)} %param.13) | copy-start | bytes 196

commit v5 on v4

--- a/solution.py
+++ b/solution.py
@@ -22,7 +22,7 @@
 
 NT = (((1,), (1,)), ((), ()))
 MIB = 1 << 20
-PITCH = 72
+PITCH = 136
 STEP = 136
 
 
@@ -113,7 +113,7 @@
             for u in range(8):
                 turned[r, h, u * STEP : u * STEP + 128, :] = landed[r, h, u].T
             for ch in range(CH):
-                o_ref[ch % 64, ch // 64, r, h] = turned[r, h, pl.ds(ch, 8, stride=STEP), :]
+                o_ref[ch % 32, r, ch // 32, h] = turned[r, h, pl.ds(ch, 8, stride=STEP), :]
 
 
 def pack(samples):
@@ -122,7 +122,7 @@
         pack_kernel,
         in_specs=[pl.BlockSpec(memory_space=pltpu.HBM)],
         out_specs=pl.BlockSpec(memory_space=pltpu.VMEM),
-        out_shape=jax.ShapeDtypeStruct((64, 2, 2, 2, 8, 128), jnp.float32),
+        out_shape=jax.ShapeDtypeStruct((32, 2, 4, 2, 8, 128), jnp.float32),
         scratch_shapes=[
             pltpu.VMEM((2, 2, 8, 128, CH), jnp.float32),
             pltpu.VMEM((2, 2, 9 * STEP, 128), jnp.float32),
@@ -141,7 +141,7 @@
     upper = lax.broadcasted_iota(jnp.int32, (32, 8, 128), 1) < 4
 
     for i in range(4):
-        halves = [x_ref[:, i // 2, i % 2, h].reshape(T1, 128) for h in range(2)]
+        halves = [x_ref[:, i, h].reshape(T1, 128) for h in range(2)]
         x = jnp.concatenate(halves, axis=1) * w_ref[...]
         xh, xl = split(x[:256] + x[256:])
         a_even = dot(fe_ref[...], jnp.concatenate([xh, xl, xh], axis=0))
@@ -208,14 +208,14 @@
 def cross_kernel(x_ref, o_ref, rows, *, scale):
     row = lax.broadcasted_iota(jnp.int32, (CH, CH), 0)
     col = lax.broadcasted_iota(jnp.int32, (CH, CH), 1)
-    for q in range(64):
-        rows[q * PITCH : q * PITCH + 64, :] = x_ref[q * 64 : q * 64 + 64, :]
-    for r in range(2):
+    for chip in range(32):
+        rows[chip * PITCH : chip * PITCH + 128, :] = x_ref[chip * 128 : chip * 128 + 128, :]
+    for band in range(2):
         parts = []
         for part in range(2):
-            for c in range(2):
+            for c in range(4):
                 cols = [
-                    rows[pl.ds((c * 2 + r) * 16 + half * 8 + part * 2 + m, 64, stride=PITCH), :]
+                    rows[pl.ds((band * 4 + c) * 16 + half * 8 + part * 2 + m, 32, stride=PITCH), :]
                     for m in (0, 1, 4, 5)
                     for half in range(2)
                 ]
@@ -228,7 +228,7 @@
         imag = g[CH:, :CH] - g[:CH, CH:]
         packed = jnp.where(row >= col, real, imag) * scale
         for y in range(8):
-            o_ref[y, r] = packed
+            o_ref[band * 8 + y] = packed
 
 
 def cross(x):
@@ -237,8 +237,8 @@
         functools.partial(cross_kernel, scale=scale),
         in_specs=[pl.BlockSpec(memory_space=pltpu.VMEM)],
         out_specs=pl.BlockSpec(memory_space=pltpu.VMEM),
-        out_shape=jax.ShapeDtypeStruct((8, 2, CH, CH), jnp.float32),
-        scratch_shapes=[pltpu.VMEM((65 * PITCH, 128), jnp.float32)],
+        out_shape=jax.ShapeDtypeStruct((16, CH, CH), jnp.float32),
+        scratch_shapes=[pltpu.VMEM((33 * PITCH, 128), jnp.float32)],
         compiler_params=pltpu.CompilerParams(vmem_limit_bytes=24 * MIB),
         name="cross",
     )(x.reshape(64 * 64, 128))
@@ -250,8 +250,9 @@
     row = lax.broadcasted_iota(jnp.int32, (CH, CH), 0)
     col = lax.broadcasted_iota(jnp.int32, (CH, CH), 1)
     levels, turns = lev_vec[...], roll_vec[...]
-    lev_ref = [levels[0, r] for r in range(RUNS)]
-    roll_ref = [turns[0, r] for r in range(RUNS)]
+    order = [2 * (k % 8) + k // 8 for k in range(RUNS)]
+    lev_ref = [levels[0, r] for r in order]
+    roll_ref = [turns[0, r] for r in order]
     sums[...] = jnp.zeros_like(sums)
     rolls[...] = jnp.zeros_like(rolls)
     squares[...] = jnp.zeros_like(squares)
@@ -314,18 +315,22 @@
         + [pltpu.SemaphoreType.DMA((3, 4))],
         compiler_params=pltpu.CompilerParams(vmem_limit_bytes=16 * MIB),
         name="moments",
-    )(cohesion.reshape(1, RUNS), rolling.reshape(1, RUNS), x.reshape(RUNS, CH, CH))
-
-
-def exchange(x, axis):
-    return lax.all_to_all(x, axis, split_axis=0, concat_axis=0, tiled=True)
+    )(cohesion.reshape(1, RUNS), rolling.reshape(1, RUNS), x)
+
+
+def exchange(x, axis, groups=None):
+    return lax.all_to_all(
+        x, axis, split_axis=0, concat_axis=0, tiled=True, axis_index_groups=groups
+    )
 
 
 def per_device(samples, cohesion, rolling):
+    same_core = [[2 * chip + core for chip in range(32)] for core in range(2)]
+    column = [[16 * chip + k for k in range(16)] for chip in range(32)]
     series = exchange(pack(samples).reshape(64, 64, 128), "tm")
-    bins = dft(series.reshape(64, 2, 2, 2, 8, 128))
-    band = exchange(bins.reshape(64, 64, 128), "tm")
-    gathered = exchange(cross(band), "runs")
+    bins = dft(series.reshape(64, 4, 2, 8, 128))
+    bands = exchange(bins.reshape(32, 128, 128), "tm", same_core)
+    gathered = exchange(cross(bands), ("tm", "runs"), column)
     return moments(cohesion, rolling, gathered)
 
 

time: 165 us -> 164 us (level)
  the two profiles are of different devices: /device:TPU:4 before, /device:TPU:10 now
where the time goes in v5:
time: 164 us
  blocking collectives  156 us (95%)
  Pallas kernels  7.61 us (5%)
    all_to_all x3, blocking collectives, exchange(): lax.all_to_all(x, axis, split_axis=0, concat_axis=0, tiled=True, axis_ind...  156 us

profile of v5, /device:TPU:10, one launch (start us, length us, event | category | flops | bytes accessed | tf_op | source)
XLA Modules:
  0.0 163.9 jit_solution(12333198421948480922)
XLA Ops:
  0.6 2.1 %pack.1 = f32[32,2,4,2,8,128]{5,4,3,2,1,0:T(8,128)S(1)} custom-call(f32[2,8,2,128,128]{4,3,2,1,0:T(8,128)} %bitcast.13), custom_call_target="tpu_custom_call" | custom-call | tf_op jit(solution)/shard_map/pack/pallas_call | solution.py:121
  2.8 0.0 copy-start
  2.8 0.0 copy-start.1
  2.8 0.0 copy-start.2
  2.8 0.0 copy-start.3
  2.8 0.0 copy-start.4
  2.8 0.0 copy-start.5
  2.9 0.0 copy-start.6
  2.9 0.0 copy-start.7
  2.9 65.2 %all_to_all.15 = f32[64,64,128]{2,1,0:T(8,128)S(1)} all-to-all(f32[64,64,128]{2,1,0:T(8,128)S(1)} %bitcast.8), channel_id=1, replica_groups=mesh['tm'=64,'runs'=8] {'tm'}, dimensions={0} | all-to-all | bytes 4194304 | tf_op jit(solution)/shard_map/all_to_all | solution.py:322
  68.1 0.0 copy-done
  68.1 0.0 copy-done.1
  68.1 0.0 copy-done.2
  68.1 0.0 copy-done.3
  68.1 0.0 copy-done.4
  68.1 0.0 copy-done.5
  68.1 0.0 copy-done.6
  68.1 0.0 copy-done.7
  68.1 2.6 %dft.1 = f32[32,2,4,2,8,128]{5,4,3,2,1,0:T(8,128)S(1)} custom-call(f32[64,4,2,8,128]{4,3,2,1,0:T(8,128)S(1)} %bitcast.9, f32[512,256]{1,0:T(8,128)S(1)} %copy-done.1, f32[256,256]{1,0:T(8,128)S(1)} %copy-done.7, f32[256,256]{1,0:T(8,128)S(1)} %copy-done.6, bf16[256,768]{1,0:T(8,128)(2,1)S(1)} %copy-done.5, bf16[256,768]{1,0:T(8,128)(2,1)S(1)} %copy-done.4, ...), custom_call_target="tpu_custom_call" | custom-call | tf_op jit(solution)/shard_map/dft/pallas_call | solution.py:194
  70.7 55.3 %all_to_all.16 = f32[32,128,128]{2,1,0:T(8,128)S(1)} all-to-all(f32[32,128,128]{2,1,0:T(8,128)S(1)} %bitcast.10), channel_id=1, replica_groups={{0,16,32,48,64,80,96,112,128,144,160,176,192,208,224,240,256,272,288,30..., dimensions={0} | all-to-all | bytes 4194304 | tf_op jit(solution)/shard_map/all_to_all | solution.py:322
  126.1 1.0 cross.1
  127.1 35.0 %all_to_all.17.x_ref = f32[16,128,128]{2,1,0:T(8,128)S(1)} all-to-all(f32[16,128,128]{2,1,0:T(8,128)S(1)} %cross.1), channel_id=1, replica_groups={{0,1,2,3,4,5,6,7,8,9,10,11,12,13,14,15},{16,17,18,19,20,21,22,23,24,25,..., dimensions={0} | all-to-all | bytes 2097152 | tf_op jit(solution)/shard_map/all_to_all | solution.py:322
  162.1 0.0 copy-done.9
  162.1 1.8 %moments.1 = (f32[4,1,2,128,128]{4,3,2,1,0:T(8,128)}, f32[4,1,128,128]{3,2,1,0:T(8,128)}, f32[4,1,2,128,128]{4,3,2,1,0:T(8,128)}) custom-call(s32[1,16]{1,0:T(1,128)S(1)} %bitcast.11, s32[1,16]{1,0:T(1,128)S(1)} %bitcast.12, f32[16,128,128]{2,1,0:T(8,128)S(1)} %all_to_all.17.x_ref), custom_call_target="tpu_custom_call" | custom-call | tf_op jit(solution)/shard_map/moments/pallas_call | solution.py:308
  (3 shorter events, 0.0 us)
Async XLA Ops:
  2.8 65.3 %copy-start = (bf16[512,768]{1,0:T(8,128)(2,1)S(1)}, bf16[512,768]{1,0:T(8,128)(2,1)}, u32[]{:S(2)}) copy-start(bf16[512,768]{1,0:T(8,128)(2,1)} %constant.23.clone.edge_ref) | copy-start | bytes 2359300
  2.8 65.3 %copy-start.1 = (f32[512,256]{1,0:T(8,128)S(1)}, f32[512,256]{1,0:T(8,128)}, u32[]{:S(2)}) copy-start(f32[512,256]{1,0:T(8,128)} %constant.16.clone.w_ref) | copy-start | bytes 1572868
  2.8 65.3 %copy-start.2 = (bf16[256,768]{1,0:T(8,128)(2,1)S(1)}, bf16[256,768]{1,0:T(8,128)(2,1)}, u32[]{:S(2)}) copy-start(bf16[256,768]{1,0:T(8,128)(2,1)} %constant.22.clone.so_ref) | copy-start | bytes 1179652
  2.8 65.3 %copy-start.3 = (bf16[256,768]{1,0:T(8,128)(2,1)S(1)}, bf16[256,768]{1,0:T(8,128)(2,1)}, u32[]{:S(2)}) copy-start(bf16[256,768]{1,0:T(8,128)(2,1)} %constant.21.clone.se_ref) | copy-start | bytes 1179652
  2.8 65.3 %copy-start.4 = (bf16[256,768]{1,0:T(8,128)(2,1)S(1)}, bf16[256,768]{1,0:T(8,128)(2,1)}, u32[]{:S(2)}) copy-start(bf16[256,768]{1,0:T(8,128)(2,1)} %constant.20.clone.fo_ref) | copy-start | bytes 1179652
  2.8 65.3 %copy-start.5 = (bf16[256,768]{1,0:T(8,128)(2,1)S(1)}, bf16[256,768]{1,0:T(8,128)(2,1)}, u32[]{:S(2)}) copy-start(bf16[256,768]{1,0:T(8,128)(2,1)} %constant.19.clone.fe_ref) | copy-start | bytes 1179652
  2.9 65.3 %copy-start.6 = (f32[256,256]{1,0:T(8,128)S(1)}, f32[256,256]{1,0:T(8,128)}, u32[]{:S(2)}) copy-start(f32[256,256]{1,0:T(8,128)} %constant.18.clone.s_ref) | copy-start | bytes 786436
  2.9 65.3 %copy-start.7 = (f32[256,256]{1,0:T(8,128)S(1)}, f32[256,256]{1,0:T(8,128)}, u32[]{:S(2)}) copy-start(f32[256,256]{1,0:T(8,128)} %constant.17.clone.c_ref) | copy-start | bytes 786436
  126.1 36.0 %copy-start.8 = (s32[16]{0:T(128)S(1)}, s32[16]{0:T(128)}, u32[]{:S(2)}) copy-start(s32[16]{0:T(128)} %param.12) | copy-start | bytes 196
  126.1 36.0 %copy-start.9 = (s32[16]{0:T(128)S(1)}, s32[16]{0:T(128)}, u32[]{:S(2)}) copy-start(s32[16]{0:T(128)} %param.13) | copy-start | bytes 196

commit v6 on v4

--- a/solution.py
+++ b/solution.py
@@ -24,6 +24,7 @@
 MIB = 1 << 20
 PITCH = 72
 STEP = 136
+RING = [0, 5, 2, 7, 4, 1, 6, 3]
 
 
 def split_table(table):
@@ -250,8 +251,9 @@
     row = lax.broadcasted_iota(jnp.int32, (CH, CH), 0)
     col = lax.broadcasted_iota(jnp.int32, (CH, CH), 1)
     levels, turns = lev_vec[...], roll_vec[...]
-    lev_ref = [levels[0, r] for r in range(RUNS)]
-    roll_ref = [turns[0, r] for r in range(RUNS)]
+    order = [2 * y + r for y in RING for r in range(2)]
+    lev_ref = [levels[0, r] for r in order]
+    roll_ref = [turns[0, r] for r in order]
     sums[...] = jnp.zeros_like(sums)
     rolls[...] = jnp.zeros_like(rolls)
     squares[...] = jnp.zeros_like(squares)
@@ -317,15 +319,17 @@
     )(cohesion.reshape(1, RUNS), rolling.reshape(1, RUNS), x.reshape(RUNS, CH, CH))
 
 
-def exchange(x, axis):
-    return lax.all_to_all(x, axis, split_axis=0, concat_axis=0, tiled=True)
+def exchange(x, axis, groups=None):
+    return lax.all_to_all(
+        x, axis, split_axis=0, concat_axis=0, tiled=True, axis_index_groups=groups
+    )
 
 
 def per_device(samples, cohesion, rolling):
     series = exchange(pack(samples).reshape(64, 64, 128), "tm")
     bins = dft(series.reshape(64, 2, 2, 2, 8, 128))
     band = exchange(bins.reshape(64, 64, 128), "tm")
-    gathered = exchange(cross(band), "runs")
+    gathered = exchange(cross(band), "runs", [RING])
     return moments(cohesion, rolling, gathered)
 
 

time: 165 us -> 165 us (level)
  no operation moved by 1% of the time
where the time goes in v6:
time: 165 us
  blocking collectives  156 us (95%)
  Pallas kernels  7.61 us (5%)
    all_to_all x3, blocking collectives, exchange(): lax.all_to_all(x, axis, split_axis=0, concat_axis=0, tiled=True, axis_ind...  156 us

profile of v6, /device:TPU:4, one launch (start us, length us, event | category | flops | bytes accessed | tf_op | source)
XLA Modules:
  0.0 164.7 jit_solution(5237731983775038155)
XLA Ops:
  0.6 2.1 %pack.1 = f32[64,2,2,2,8,128]{5,4,3,2,1,0:T(8,128)S(1)} custom-call(f32[2,8,2,128,128]{4,3,2,1,0:T(8,128)} %bitcast.15), custom_call_target="tpu_custom_call" | custom-call | tf_op jit(solution)/shard_map/pack/pallas_call | solution.py:122
  2.8 0.0 copy-start
  2.8 0.0 copy-start.1
  2.8 0.0 copy-start.2
  2.8 0.0 copy-start.3
  2.8 0.0 copy-start.4
  2.8 0.0 copy-start.5
  2.9 0.0 copy-start.6
  2.9 0.0 copy-start.7
  2.9 65.2 %all_to_all.15 = f32[64,64,128]{2,1,0:T(8,128)S(1)} all-to-all(f32[64,64,128]{2,1,0:T(8,128)S(1)} %bitcast.9), channel_id=1, replica_groups=mesh['tm'=64,'runs'=8] {'tm'}, dimensions={0} | all-to-all | bytes 4194304 | tf_op jit(solution)/shard_map/all_to_all | solution.py:323
  68.1 0.0 copy-done
  68.1 0.0 copy-done.1
  68.1 0.0 copy-done.2
  68.1 0.0 copy-done.3
  68.1 0.0 copy-done.4
  68.1 0.0 copy-done.5
  68.1 0.0 copy-done.6
  68.1 0.0 copy-done.7
  68.1 2.6 %dft.1 = f32[32,2,4,2,8,128]{5,4,3,2,1,0:T(8,128)S(1)} custom-call(f32[64,2,2,2,8,128]{5,4,3,2,1,0:T(8,128)S(1)} %bitcast.10, f32[512,256]{1,0:T(8,128)S(1)} %copy-done.1, f32[256,256]{1,0:T(8,128)S(1)} %copy-done.7, f32[256,256]{1,0:T(8,128)S(1)} %copy-done.6, bf16[256,768]{1,0:T(8,128)(2,1)S(1)} %copy-done.5, bf16[256,768]{1,0:T(8,128)(2,1)S(1)} %copy-done.4, ...), custom_call_target="tpu_custom_call" | custom-call | tf_op jit(solution)/shard_map/dft/pallas_call | solution.py:195
  70.7 56.5 %all_to_all.16 = f32[64,64,128]{2,1,0:T(8,128)S(1)} all-to-all(f32[64,64,128]{2,1,0:T(8,128)S(1)} %bitcast.11), channel_id=1, replica_groups=mesh['tm'=64,'runs'=8] {'tm'}, dimensions={0} | all-to-all | bytes 4194304 | tf_op jit(solution)/shard_map/all_to_all | solution.py:323
  127.2 1.0 cross.1
  128.3 34.6 %all_to_all.17 = f32[8,2,128,128]{3,2,1,0:T(8,128)S(1)} all-to-all(f32[8,2,128,128]{3,2,1,0:T(8,128)S(1)} %cross.1), channel_id=1, replica_groups={{0,5,2,7,4,1,6,3},{8,13,10,15,12,9,14,11},{16,21,18,23,20,17,22,19},{24..., dimensions={0} | all-to-all | bytes 2097152 | tf_op jit(solution)/shard_map/all_to_all | solution.py:323
  162.9 0.0 copy-done.8
  162.9 1.8 %moments.1 = (f32[4,1,2,128,128]{4,3,2,1,0:T(8,128)}, f32[4,1,128,128]{3,2,1,0:T(8,128)}, f32[4,1,2,128,128]{4,3,2,1,0:T(8,128)}) custom-call(s32[1,16]{1,0:T(1,128)S(1)} %bitcast.13, s32[1,16]{1,0:T(1,128)S(1)} %bitcast.14, f32[16,128,128]{2,1,0:T(8,128)S(1)} %bitcast.12), custom_call_target="tpu_custom_call" | custom-call | tf_op jit(solution)/shard_map/moments/pallas_call | solution.py:309
  (3 shorter events, 0.0 us)
Async XLA Ops:
  2.8 65.3 %copy-start = (bf16[512,768]{1,0:T(8,128)(2,1)S(1)}, bf16[512,768]{1,0:T(8,128)(2,1)}, u32[]{:S(2)}) copy-start(bf16[512,768]{1,0:T(8,128)(2,1)} %constant.23.clone.edge_ref) | copy-start | bytes 2359300
  2.8 65.3 %copy-start.1 = (f32[512,256]{1,0:T(8,128)S(1)}, f32[512,256]{1,0:T(8,128)}, u32[]{:S(2)}) copy-start(f32[512,256]{1,0:T(8,128)} %constant.16.clone.w_ref) | copy-start | bytes 1572868
  2.8 65.3 %copy-start.2 = (bf16[256,768]{1,0:T(8,128)(2,1)S(1)}, bf16[256,768]{1,0:T(8,128)(2,1)}, u32[]{:S(2)}) copy-start(bf16[256,768]{1,0:T(8,128)(2,1)} %constant.22.clone.so_ref) | copy-start | bytes 1179652
  2.8 65.3 %copy-start.3 = (bf16[256,768]{1,0:T(8,128)(2,1)S(1)}, bf16[256,768]{1,0:T(8,128)(2,1)}, u32[]{:S(2)}) copy-start(bf16[256,768]{1,0:T(8,128)(2,1)} %constant.21.clone.se_ref) | copy-start | bytes 1179652
  2.8 65.3 %copy-start.4 = (bf16[256,768]{1,0:T(8,128)(2,1)S(1)}, bf16[256,768]{1,0:T(8,128)(2,1)}, u32[]{:S(2)}) copy-start(bf16[256,768]{1,0:T(8,128)(2,1)} %constant.20.clone.fo_ref) | copy-start | bytes 1179652
  2.8 65.2 %copy-start.5 = (bf16[256,768]{1,0:T(8,128)(2,1)S(1)}, bf16[256,768]{1,0:T(8,128)(2,1)}, u32[]{:S(2)}) copy-start(bf16[256,768]{1,0:T(8,128)(2,1)} %constant.19.clone.fe_ref) | copy-start | bytes 1179652
  2.9 65.2 %copy-start.6 = (f32[256,256]{1,0:T(8,128)S(1)}, f32[256,256]{1,0:T(8,128)}, u32[]{:S(2)}) copy-start(f32[256,256]{1,0:T(8,128)} %constant.18.clone.s_ref) | copy-start | bytes 786436
  2.9 65.2 %copy-start.7 = (f32[256,256]{1,0:T(8,128)S(1)}, f32[256,256]{1,0:T(8,128)}, u32[]{:S(2)}) copy-start(f32[256,256]{1,0:T(8,128)} %constant.17.clone.c_ref) | copy-start | bytes 786436
  127.2 35.7 %copy-start.8 = (s32[16]{0:T(128)S(1)}, s32[16]{0:T(128)}, u32[]{:S(2)}) copy-start(s32[16]{0:T(128)} %param.12) | copy-start | bytes 196
  127.2 35.7 %copy-start.9 = (s32[16]{0:T(128)S(1)}, s32[16]{0:T(128)}, u32[]{:S(2)}) copy-start(s32[16]{0:T(128)} %param.13) | copy-start | bytes 196

commit v7 on v4

--- a/solution.py
+++ b/solution.py
@@ -172,9 +172,13 @@
 
     for i in range(4):
         bh, bl = middle[i, 0, 0], middle[i, 0, 1]
-        o_even = dot_nt(se_ref[...], jnp.concatenate([bh, bl, bh], axis=1))
+        o_even = dot_nt(se_ref[:, :256], bl) + dot_nt(
+            se_ref[:, 256:], jnp.concatenate([bh, bh], axis=1)
+        )
         bh, bl = middle[i, 1, 0], middle[i, 1, 1]
-        o_odd = dot_nt(so_ref[...], jnp.concatenate([bh, bl, bh], axis=1))
+        o_odd = dot_nt(so_ref[:, :256], bl) + dot_nt(
+            so_ref[:, 256:], jnp.concatenate([bh, bh], axis=1)
+        )
         low = edge if i == 0 else pltpu.roll(edge, 128 - i, 1)
         extra = jnp.where(sub, low, pltpu.roll(edge, 124 - i, 1))
         extra = jnp.where(first_lane, extra, 0.0).reshape(32, 2, 8, 128)
@@ -262,11 +266,9 @@
         imag = jnp.where(row < col, m, jnp.where(row > col, -t, 0.0))
         return real, imag
 
-    def count(ref, level):
-        total = jnp.int32(0)
-        for r in range(RUNS):
-            total += (ref[r] == level).astype(jnp.int32)
-        return jnp.maximum(total, 1).astype(jnp.float32)
+    def count(values, level):
+        total = jnp.sum((values == level).astype(jnp.float32), axis=1, keepdims=True)
+        return jnp.maximum(total, 1.0)
 
     sends = []
 
@@ -276,14 +278,14 @@
         sends.append(copy)
 
     for r in range(RUNS):
-        rolls[roll_ref[r]] += x_ref[r]
+        value = x_ref[r]
+        rolls[roll_ref[r]] += value
+        sums[lev_ref[r]] += value
     for q in range(NQ):
-        rm[q, 0, 0], rm[q, 0, 1] = unpack(rolls[q] / count(roll_ref, q))
+        rm[q, 0, 0], rm[q, 0, 1] = unpack(rolls[q] / count(turns, q))
         send(rm, rm_hbm, 0, q)
-    for r in range(RUNS):
-        sums[lev_ref[r]] += x_ref[r]
     for l in range(NC):
-        mean = sums[l] / count(lev_ref, l)
+        mean = sums[l] / count(levels, l)
         sums[l] = mean
         lm[l, 0, 0], lm[l, 0, 1] = unpack(mean)
         send(lm, lm_hbm, 1, l)

time: 165 us -> 165 us (level)
  no operation moved by 1% of the time
where the time goes in v7:
time: 165 us; the launch traced here: 164 us
  blocking collectives  156 us (95%)
  Pallas kernels  7.34 us (4%)
    all_to_all x3, blocking collectives, exchange(): return lax.all_to_all(x, axis, split_axis=0, concat_axis=0, tiled=True)  156 us

profile of v7, /device:TPU:4, one launch (start us, length us, event | category | flops | bytes accessed | tf_op | source)
XLA Modules:
  0.0 164.4 jit_solution(6631886633726045998)
XLA Ops:
  0.6 2.1 %pack.1 = f32[64,2,2,2,8,128]{5,4,3,2,1,0:T(8,128)S(1)} custom-call(f32[2,8,2,128,128]{4,3,2,1,0:T(8,128)} %bitcast.15), custom_call_target="tpu_custom_call" | custom-call | tf_op jit(solution)/shard_map/pack/pallas_call | solution.py:121
  2.8 0.0 copy-start
  2.8 0.0 copy-start.1
  2.8 0.0 copy-start.2
  2.8 0.0 copy-start.3
  2.8 0.0 copy-start.4
  2.8 0.0 copy-start.5
  2.9 0.0 copy-start.6
  2.9 0.0 copy-start.7
  2.9 65.2 %all_to_all.15 = f32[64,64,128]{2,1,0:T(8,128)S(1)} all-to-all(f32[64,64,128]{2,1,0:T(8,128)S(1)} %bitcast.9), channel_id=1, replica_groups=mesh['tm'=64,'runs'=8] {'tm'}, dimensions={0} | all-to-all | bytes 4194304 | tf_op jit(solution)/shard_map/all_to_all | solution.py:323
  68.1 0.0 copy-done
  68.1 0.0 copy-done.1
  68.1 0.0 copy-done.2
  68.1 0.0 copy-done.3
  68.1 0.0 copy-done.4
  68.1 0.0 copy-done.5
  68.1 0.0 copy-done.6
  68.1 0.0 copy-done.7
  68.1 2.5 %dft.1 = f32[32,2,4,2,8,128]{5,4,3,2,1,0:T(8,128)S(1)} custom-call(f32[64,2,2,2,8,128]{5,4,3,2,1,0:T(8,128)S(1)} %bitcast.10, f32[512,256]{1,0:T(8,128)S(1)} %copy-done.1, f32[256,256]{1,0:T(8,128)S(1)} %copy-done.7, f32[256,256]{1,0:T(8,128)S(1)} %copy-done.6, bf16[256,768]{1,0:T(8,128)(2,1)S(1)} %copy-done.5, bf16[256,768]{1,0:T(8,128)(2,1)S(1)} %copy-done.4, ...), custom_call_target="tpu_custom_call" | custom-call | tf_op jit(solution)/shard_map/dft/pallas_call | solution.py:198
  70.7 56.5 %all_to_all.16 = f32[64,64,128]{2,1,0:T(8,128)S(1)} all-to-all(f32[64,64,128]{2,1,0:T(8,128)S(1)} %bitcast.11), channel_id=1, replica_groups=mesh['tm'=64,'runs'=8] {'tm'}, dimensions={0} | all-to-all | bytes 4194304 | tf_op jit(solution)/shard_map/all_to_all | solution.py:323
  127.2 1.0 cross.1
  128.2 34.6 %all_to_all.17 = f32[8,2,128,128]{3,2,1,0:T(8,128)S(1)} all-to-all(f32[8,2,128,128]{3,2,1,0:T(8,128)S(1)} %cross.1), channel_id=1, replica_groups=mesh['tm'=64,'runs'=8] {'runs'}, dimensions={0} | all-to-all | bytes 2097152 | tf_op jit(solution)/shard_map/all_to_all | solution.py:323
  162.8 0.0 copy-done.8
  162.8 1.6 moments.1
  (3 shorter events, 0.0 us)
Async XLA Ops:
  2.8 65.3 %copy-start = (bf16[512,768]{1,0:T(8,128)(2,1)S(1)}, bf16[512,768]{1,0:T(8,128)(2,1)}, u32[]{:S(2)}) copy-start(bf16[512,768]{1,0:T(8,128)(2,1)} %constant.23.clone.edge_ref) | copy-start | bytes 2359300
  2.8 65.3 %copy-start.1 = (f32[512,256]{1,0:T(8,128)S(1)}, f32[512,256]{1,0:T(8,128)}, u32[]{:S(2)}) copy-start(f32[512,256]{1,0:T(8,128)} %constant.16.clone.w_ref) | copy-start | bytes 1572868
  2.8 65.3 %copy-start.2 = (bf16[256,768]{1,0:T(8,128)(2,1)S(1)}, bf16[256,768]{1,0:T(8,128)(2,1)}, u32[]{:S(2)}) copy-start(bf16[256,768]{1,0:T(8,128)(2,1)} %constant.22.clone.so_ref) | copy-start | bytes 1179652
  2.8 65.3 %copy-start.3 = (bf16[256,768]{1,0:T(8,128)(2,1)S(1)}, bf16[256,768]{1,0:T(8,128)(2,1)}, u32[]{:S(2)}) copy-start(bf16[256,768]{1,0:T(8,128)(2,1)} %constant.21.clone.se_ref) | copy-start | bytes 1179652
  2.8 65.3 %copy-start.4 = (bf16[256,768]{1,0:T(8,128)(2,1)S(1)}, bf16[256,768]{1,0:T(8,128)(2,1)}, u32[]{:S(2)}) copy-start(bf16[256,768]{1,0:T(8,128)(2,1)} %constant.20.clone.fo_ref) | copy-start | bytes 1179652
  2.8 65.2 %copy-start.5 = (bf16[256,768]{1,0:T(8,128)(2,1)S(1)}, bf16[256,768]{1,0:T(8,128)(2,1)}, u32[]{:S(2)}) copy-start(bf16[256,768]{1,0:T(8,128)(2,1)} %constant.19.clone.fe_ref) | copy-start | bytes 1179652
  2.9 65.2 %copy-start.6 = (f32[256,256]{1,0:T(8,128)S(1)}, f32[256,256]{1,0:T(8,128)}, u32[]{:S(2)}) copy-start(f32[256,256]{1,0:T(8,128)} %constant.18.clone.s_ref) | copy-start | bytes 786436
  2.9 65.2 %copy-start.7 = (f32[256,256]{1,0:T(8,128)S(1)}, f32[256,256]{1,0:T(8,128)}, u32[]{:S(2)}) copy-start(f32[256,256]{1,0:T(8,128)} %constant.17.clone.c_ref) | copy-start | bytes 786436
  127.1 35.7 %copy-start.8 = (s32[16]{0:T(128)S(1)}, s32[16]{0:T(128)}, u32[]{:S(2)}) copy-start(s32[16]{0:T(128)} %param.12) | copy-start | bytes 196
  127.1 35.7 %copy-start.9 = (s32[16]{0:T(128)S(1)}, s32[16]{0:T(128)}, u32[]{:S(2)}) copy-start(s32[16]{0:T(128)} %param.13) | copy-start | bytes 196

commit v8 on v5

--- a/solution.py
+++ b/solution.py
@@ -172,9 +172,13 @@
 
     for i in range(4):
         bh, bl = middle[i, 0, 0], middle[i, 0, 1]
-        o_even = dot_nt(se_ref[...], jnp.concatenate([bh, bl, bh], axis=1))
+        o_even = dot_nt(se_ref[:, :256], bl) + dot_nt(
+            se_ref[:, 256:], jnp.concatenate([bh, bh], axis=1)
+        )
         bh, bl = middle[i, 1, 0], middle[i, 1, 1]
-        o_odd = dot_nt(so_ref[...], jnp.concatenate([bh, bl, bh], axis=1))
+        o_odd = dot_nt(so_ref[:, :256], bl) + dot_nt(
+            so_ref[:, 256:], jnp.concatenate([bh, bh], axis=1)
+        )
         low = edge if i == 0 else pltpu.roll(edge, 128 - i, 1)
         extra = jnp.where(sub, low, pltpu.roll(edge, 124 - i, 1))
         extra = jnp.where(first_lane, extra, 0.0).reshape(32, 2, 8, 128)
@@ -263,11 +267,9 @@
         imag = jnp.where(row < col, m, jnp.where(row > col, -t, 0.0))
         return real, imag
 
-    def count(ref, level):
-        total = jnp.int32(0)
-        for r in range(RUNS):
-            total += (ref[r] == level).astype(jnp.int32)
-        return jnp.maximum(total, 1).astype(jnp.float32)
+    def count(values, level):
+        total = jnp.sum((values == level).astype(jnp.float32), axis=1, keepdims=True)
+        return jnp.maximum(total, 1.0)
 
     sends = []
 
@@ -277,14 +279,14 @@
         sends.append(copy)
 
     for r in range(RUNS):
-        rolls[roll_ref[r]] += x_ref[r]
+        value = x_ref[r]
+        rolls[roll_ref[r]] += value
+        sums[lev_ref[r]] += value
     for q in range(NQ):
-        rm[q, 0, 0], rm[q, 0, 1] = unpack(rolls[q] / count(roll_ref, q))
+        rm[q, 0, 0], rm[q, 0, 1] = unpack(rolls[q] / count(turns, q))
         send(rm, rm_hbm, 0, q)
-    for r in range(RUNS):
-        sums[lev_ref[r]] += x_ref[r]
     for l in range(NC):
-        mean = sums[l] / count(lev_ref, l)
+        mean = sums[l] / count(levels, l)
         sums[l] = mean
         lm[l, 0, 0], lm[l, 0, 1] = unpack(mean)
         send(lm, lm_hbm, 1, l)

time: 164 us -> 164 us (level)
  no operation moved by 1% of the time
where the time goes in v8:
time: 164 us
  blocking collectives  156 us (95%)
  Pallas kernels  7.32 us (4%)
    all_to_all x3, blocking collectives, exchange(): lax.all_to_all(x, axis, split_axis=0, concat_axis=0, tiled=True, axis_ind...  156 us

profile of v8, /device:TPU:10, one launch (start us, length us, event | category | flops | bytes accessed | tf_op | source)
XLA Modules:
  0.0 163.7 jit_solution(6895474830836536098)
XLA Ops:
  0.6 2.1 %pack.1 = f32[32,2,4,2,8,128]{5,4,3,2,1,0:T(8,128)S(1)} custom-call(f32[2,8,2,128,128]{4,3,2,1,0:T(8,128)} %bitcast.13), custom_call_target="tpu_custom_call" | custom-call | tf_op jit(solution)/shard_map/pack/pallas_call | solution.py:121
  2.8 0.0 copy-start
  2.8 0.0 copy-start.1
  2.8 0.0 copy-start.2
  2.8 0.0 copy-start.3
  2.8 0.0 copy-start.4
  2.8 0.0 copy-start.5
  2.9 0.0 copy-start.6
  2.9 0.0 copy-start.7
  2.9 65.2 %all_to_all.15 = f32[64,64,128]{2,1,0:T(8,128)S(1)} all-to-all(f32[64,64,128]{2,1,0:T(8,128)S(1)} %bitcast.8), channel_id=1, replica_groups=mesh['tm'=64,'runs'=8] {'tm'}, dimensions={0} | all-to-all | bytes 4194304 | tf_op jit(solution)/shard_map/all_to_all | solution.py:324
  68.1 0.0 copy-done
  68.1 0.0 copy-done.1
  68.1 0.0 copy-done.2
  68.1 0.0 copy-done.3
  68.1 0.0 copy-done.4
  68.1 0.0 copy-done.5
  68.1 0.0 copy-done.6
  68.1 0.0 copy-done.7
  68.1 2.5 %dft.1 = f32[32,2,4,2,8,128]{5,4,3,2,1,0:T(8,128)S(1)} custom-call(f32[64,4,2,8,128]{4,3,2,1,0:T(8,128)S(1)} %bitcast.9, f32[512,256]{1,0:T(8,128)S(1)} %copy-done.1, f32[256,256]{1,0:T(8,128)S(1)} %copy-done.7, f32[256,256]{1,0:T(8,128)S(1)} %copy-done.6, bf16[256,768]{1,0:T(8,128)(2,1)S(1)} %copy-done.5, bf16[256,768]{1,0:T(8,128)(2,1)S(1)} %copy-done.4, ...), custom_call_target="tpu_custom_call" | custom-call | tf_op jit(solution)/shard_map/dft/pallas_call | solution.py:198
  70.7 55.3 %all_to_all.16 = f32[32,128,128]{2,1,0:T(8,128)S(1)} all-to-all(f32[32,128,128]{2,1,0:T(8,128)S(1)} %bitcast.10), channel_id=1, replica_groups={{0,16,32,48,64,80,96,112,128,144,160,176,192,208,224,240,256,272,288,30..., dimensions={0} | all-to-all | bytes 4194304 | tf_op jit(solution)/shard_map/all_to_all | solution.py:324
  126.0 1.0 cross.1
  127.1 35.0 %all_to_all.17.x_ref = f32[16,128,128]{2,1,0:T(8,128)S(1)} all-to-all(f32[16,128,128]{2,1,0:T(8,128)S(1)} %cross.1), channel_id=1, replica_groups={{0,1,2,3,4,5,6,7,8,9,10,11,12,13,14,15},{16,17,18,19,20,21,22,23,24,25,..., dimensions={0} | all-to-all | bytes 2097152 | tf_op jit(solution)/shard_map/all_to_all | solution.py:324
  162.0 0.0 copy-done.8
  162.1 1.6 moments.1
  (3 shorter events, 0.0 us)
Async XLA Ops:
  2.8 65.3 %copy-start = (bf16[512,768]{1,0:T(8,128)(2,1)S(1)}, bf16[512,768]{1,0:T(8,128)(2,1)}, u32[]{:S(2)}) copy-start(bf16[512,768]{1,0:T(8,128)(2,1)} %constant.23.clone.edge_ref) | copy-start | bytes 2359300
  2.8 65.3 %copy-start.1 = (f32[512,256]{1,0:T(8,128)S(1)}, f32[512,256]{1,0:T(8,128)}, u32[]{:S(2)}) copy-start(f32[512,256]{1,0:T(8,128)} %constant.16.clone.w_ref) | copy-start | bytes 1572868
  2.8 65.3 %copy-start.2 = (bf16[256,768]{1,0:T(8,128)(2,1)S(1)}, bf16[256,768]{1,0:T(8,128)(2,1)}, u32[]{:S(2)}) copy-start(bf16[256,768]{1,0:T(8,128)(2,1)} %constant.22.clone.so_ref) | copy-start | bytes 1179652
  2.8 65.3 %copy-start.3 = (bf16[256,768]{1,0:T(8,128)(2,1)S(1)}, bf16[256,768]{1,0:T(8,128)(2,1)}, u32[]{:S(2)}) copy-start(bf16[256,768]{1,0:T(8,128)(2,1)} %constant.21.clone.se_ref) | copy-start | bytes 1179652
  2.8 65.3 %copy-start.4 = (bf16[256,768]{1,0:T(8,128)(2,1)S(1)}, bf16[256,768]{1,0:T(8,128)(2,1)}, u32[]{:S(2)}) copy-start(bf16[256,768]{1,0:T(8,128)(2,1)} %constant.20.clone.fo_ref) | copy-start | bytes 1179652
  2.8 65.3 %copy-start.5 = (bf16[256,768]{1,0:T(8,128)(2,1)S(1)}, bf16[256,768]{1,0:T(8,128)(2,1)}, u32[]{:S(2)}) copy-start(bf16[256,768]{1,0:T(8,128)(2,1)} %constant.19.clone.fe_ref) | copy-start | bytes 1179652
  2.9 65.3 %copy-start.6 = (f32[256,256]{1,0:T(8,128)S(1)}, f32[256,256]{1,0:T(8,128)}, u32[]{:S(2)}) copy-start(f32[256,256]{1,0:T(8,128)} %constant.18.clone.s_ref) | copy-start | bytes 786436
  2.9 65.3 %copy-start.7 = (f32[256,256]{1,0:T(8,128)S(1)}, f32[256,256]{1,0:T(8,128)}, u32[]{:S(2)}) copy-start(f32[256,256]{1,0:T(8,128)} %constant.17.clone.c_ref) | copy-start | bytes 786436
  126.0 36.0 %copy-start.8 = (s32[16]{0:T(128)S(1)}, s32[16]{0:T(128)}, u32[]{:S(2)}) copy-start(s32[16]{0:T(128)} %param.12) | copy-start | bytes 196
  126.0 36.0 %copy-start.9 = (s32[16]{0:T(128)S(1)}, s32[16]{0:T(128)}, u32[]{:S(2)}) copy-start(s32[16]{0:T(128)} %param.13) | copy-start | bytes 196

commit v9 on v8

--- a/solution.py
+++ b/solution.py
@@ -144,9 +144,13 @@
         halves = [x_ref[:, i, h].reshape(T1, 128) for h in range(2)]
         x = jnp.concatenate(halves, axis=1) * w_ref[...]
         xh, xl = split(x[:256] + x[256:])
-        a_even = dot(fe_ref[...], jnp.concatenate([xh, xl, xh], axis=0))
+        a_even = dot(fe_ref[:, :256], xl) + dot(
+            fe_ref[:, 256:], jnp.concatenate([xh, xh], axis=0)
+        )
         xh, xl = split(x[:256] - x[256:])
-        a_odd = dot(fo_ref[...], jnp.concatenate([xh, xl, xh], axis=0))
+        a_odd = dot(fo_ref[:, :256], xl) + dot(
+            fo_ref[:, 256:], jnp.concatenate([xh, xh], axis=0)
+        )
         a_re = jnp.concatenate([a_even[:128], a_odd[:128]], axis=0)
         a_im = jnp.concatenate([a_even[128:], a_odd[128:]], axis=0)
         c, s = c_ref[...], s_ref[...]

time: 164 us -> 164 us (level)
  no operation moved by 1% of the time
where the time goes in v9:
time: 164 us
  blocking collectives  156 us (95%)
  Pallas kernels  7.45 us (5%)
    all_to_all x3, blocking collectives, exchange(): lax.all_to_all(x, axis, split_axis=0, concat_axis=0, tiled=True, axis_ind...  156 us

profile of v9, /device:TPU:10, one launch (start us, length us, event | category | flops | bytes accessed | tf_op | source)
XLA Modules:
  0.0 163.8 jit_solution(18109418801288479612)
XLA Ops:
  0.6 2.1 %pack.1 = f32[32,2,4,2,8,128]{5,4,3,2,1,0:T(8,128)S(1)} custom-call(f32[2,8,2,128,128]{4,3,2,1,0:T(8,128)} %bitcast.13), custom_call_target="tpu_custom_call" | custom-call | tf_op jit(solution)/shard_map/pack/pallas_call | solution.py:121
  2.8 0.0 copy-start
  2.8 0.0 copy-start.1
  2.8 0.0 copy-start.2
  2.8 0.0 copy-start.3
  2.8 0.0 copy-start.4
  2.8 0.0 copy-start.5
  2.9 0.0 copy-start.6
  2.9 0.0 copy-start.7
  2.9 65.2 %all_to_all.15 = f32[64,64,128]{2,1,0:T(8,128)S(1)} all-to-all(f32[64,64,128]{2,1,0:T(8,128)S(1)} %bitcast.8), channel_id=1, replica_groups=mesh['tm'=64,'runs'=8] {'tm'}, dimensions={0} | all-to-all | bytes 4194304 | tf_op jit(solution)/shard_map/all_to_all | solution.py:328
  68.1 0.0 copy-done
  68.1 0.0 copy-done.1
  68.1 0.0 copy-done.2
  68.1 0.0 copy-done.3
  68.1 0.0 copy-done.4
  68.1 0.0 copy-done.5
  68.1 0.0 copy-done.6
  68.1 0.0 copy-done.7
  68.1 2.6 %dft.1 = f32[32,2,4,2,8,128]{5,4,3,2,1,0:T(8,128)S(1)} custom-call(f32[64,4,2,8,128]{4,3,2,1,0:T(8,128)S(1)} %bitcast.9, f32[512,256]{1,0:T(8,128)S(1)} %copy-done.1, f32[256,256]{1,0:T(8,128)S(1)} %copy-done.7, f32[256,256]{1,0:T(8,128)S(1)} %copy-done.6, bf16[256,768]{1,0:T(8,128)(2,1)S(1)} %copy-done.5, bf16[256,768]{1,0:T(8,128)(2,1)S(1)} %copy-done.4, ...), custom_call_target="tpu_custom_call" | custom-call | tf_op jit(solution)/shard_map/dft/pallas_call | solution.py:202
  70.8 55.3 %all_to_all.16 = f32[32,128,128]{2,1,0:T(8,128)S(1)} all-to-all(f32[32,128,128]{2,1,0:T(8,128)S(1)} %bitcast.10), channel_id=1, replica_groups={{0,16,32,48,64,80,96,112,128,144,160,176,192,208,224,240,256,272,288,30..., dimensions={0} | all-to-all | bytes 4194304 | tf_op jit(solution)/shard_map/all_to_all | solution.py:328
  126.1 1.0 cross.1
  127.2 35.0 %all_to_all.17.x_ref = f32[16,128,128]{2,1,0:T(8,128)S(1)} all-to-all(f32[16,128,128]{2,1,0:T(8,128)S(1)} %cross.1), channel_id=1, replica_groups={{0,1,2,3,4,5,6,7,8,9,10,11,12,13,14,15},{16,17,18,19,20,21,22,23,24,25,..., dimensions={0} | all-to-all | bytes 2097152 | tf_op jit(solution)/shard_map/all_to_all | solution.py:328
  162.2 0.0 copy-done.9
  162.2 1.6 moments.1
  (3 shorter events, 0.0 us)
Async XLA Ops:
  2.8 65.3 %copy-start = (bf16[512,768]{1,0:T(8,128)(2,1)S(1)}, bf16[512,768]{1,0:T(8,128)(2,1)}, u32[]{:S(2)}) copy-start(bf16[512,768]{1,0:T(8,128)(2,1)} %constant.23.clone.edge_ref) | copy-start | bytes 2359300
  2.8 65.3 %copy-start.1 = (f32[512,256]{1,0:T(8,128)S(1)}, f32[512,256]{1,0:T(8,128)}, u32[]{:S(2)}) copy-start(f32[512,256]{1,0:T(8,128)} %constant.16.clone.w_ref) | copy-start | bytes 1572868
  2.8 65.3 %copy-start.2 = (bf16[256,768]{1,0:T(8,128)(2,1)S(1)}, bf16[256,768]{1,0:T(8,128)(2,1)}, u32[]{:S(2)}) copy-start(bf16[256,768]{1,0:T(8,128)(2,1)} %constant.22.clone.so_ref) | copy-start | bytes 1179652
  2.8 65.3 %copy-start.3 = (bf16[256,768]{1,0:T(8,128)(2,1)S(1)}, bf16[256,768]{1,0:T(8,128)(2,1)}, u32[]{:S(2)}) copy-start(bf16[256,768]{1,0:T(8,128)(2,1)} %constant.21.clone.se_ref) | copy-start | bytes 1179652
  2.8 65.3 %copy-start.4 = (bf16[256,768]{1,0:T(8,128)(2,1)S(1)}, bf16[256,768]{1,0:T(8,128)(2,1)}, u32[]{:S(2)}) copy-start(bf16[256,768]{1,0:T(8,128)(2,1)} %constant.20.clone.fo_ref) | copy-start | bytes 1179652
  2.8 65.3 %copy-start.5 = (bf16[256,768]{1,0:T(8,128)(2,1)S(1)}, bf16[256,768]{1,0:T(8,128)(2,1)}, u32[]{:S(2)}) copy-start(bf16[256,768]{1,0:T(8,128)(2,1)} %constant.19.clone.fe_ref) | copy-start | bytes 1179652
  2.9 65.3 %copy-start.6 = (f32[256,256]{1,0:T(8,128)S(1)}, f32[256,256]{1,0:T(8,128)}, u32[]{:S(2)}) copy-start(f32[256,256]{1,0:T(8,128)} %constant.18.clone.s_ref) | copy-start | bytes 786436
  2.9 65.3 %copy-start.7 = (f32[256,256]{1,0:T(8,128)S(1)}, f32[256,256]{1,0:T(8,128)}, u32[]{:S(2)}) copy-start(f32[256,256]{1,0:T(8,128)} %constant.17.clone.c_ref) | copy-start | bytes 786436
  126.1 36.0 %copy-start.8 = (s32[16]{0:T(128)S(1)}, s32[16]{0:T(128)}, u32[]{:S(2)}) copy-start(s32[16]{0:T(128)} %param.12) | copy-start | bytes 196
  126.1 36.0 %copy-start.9 = (s32[16]{0:T(128)S(1)}, s32[16]{0:T(128)}, u32[]{:S(2)}) copy-start(s32[16]{0:T(128)} %param.13) | copy-start | bytes 196

commit v10 on v9

--- a/solution.py
+++ b/solution.py
@@ -170,7 +170,9 @@
         middle[i, 1, 0], middle[i, 1, 1] = split(minus)
 
     eh, el = split(edge_in[...])
-    edge = dot_nt(edge_ref[...], jnp.concatenate([eh, el, eh], axis=1))
+    edge = dot_nt(edge_ref[:, :256], el) + dot_nt(
+        edge_ref[:, 256:], jnp.concatenate([eh, eh], axis=1)
+    )
     first_lane = lax.broadcasted_iota(jnp.int32, (512, 128), 1) == 0
     sub = lax.broadcasted_iota(jnp.int32, (512, 128), 0) % 8 < 4
 

time: 164 us -> 164 us (level)
  no operation moved by 1% of the time
where the time goes in v10:
time: 164 us
  blocking collectives  156 us (95%)
  Pallas kernels  7.43 us (5%)
    all_to_all x3, blocking collectives, exchange(): lax.all_to_all(x, axis, split_axis=0, concat_axis=0, tiled=True, axis_ind...  156 us

profile of v10, /device:TPU:10, one launch (start us, length us, event | category | flops | bytes accessed | tf_op | source)
XLA Modules:
  0.0 163.8 jit_solution(14360968383048459989)
XLA Ops:
  0.6 2.1 %pack.1 = f32[32,2,4,2,8,128]{5,4,3,2,1,0:T(8,128)S(1)} custom-call(f32[2,8,2,128,128]{4,3,2,1,0:T(8,128)} %bitcast.13), custom_call_target="tpu_custom_call" | custom-call | tf_op jit(solution)/shard_map/pack/pallas_call | solution.py:121
  2.8 0.0 copy-start
  2.8 0.0 copy-start.1
  2.8 0.0 copy-start.2
  2.8 0.0 copy-start.3
  2.8 0.0 copy-start.4
  2.8 0.0 copy-start.5
  2.9 0.0 copy-start.6
  2.9 0.0 copy-start.7
  2.9 65.2 %all_to_all.15 = f32[64,64,128]{2,1,0:T(8,128)S(1)} all-to-all(f32[64,64,128]{2,1,0:T(8,128)S(1)} %bitcast.8), channel_id=1, replica_groups=mesh['tm'=64,'runs'=8] {'tm'}, dimensions={0} | all-to-all | bytes 4194304 | tf_op jit(solution)/shard_map/all_to_all | solution.py:330
  68.1 0.0 copy-done
  68.1 0.0 copy-done.1
  68.1 0.0 copy-done.2
  68.1 0.0 copy-done.3
  68.1 0.0 copy-done.4
  68.1 0.0 copy-done.5
  68.1 0.0 copy-done.6
  68.1 0.0 copy-done.7
  68.1 2.6 %dft.1 = f32[32,2,4,2,8,128]{5,4,3,2,1,0:T(8,128)S(1)} custom-call(f32[64,4,2,8,128]{4,3,2,1,0:T(8,128)S(1)} %bitcast.9, f32[512,256]{1,0:T(8,128)S(1)} %copy-done.1, f32[256,256]{1,0:T(8,128)S(1)} %copy-done.7, f32[256,256]{1,0:T(8,128)S(1)} %copy-done.6, bf16[256,768]{1,0:T(8,128)(2,1)S(1)} %copy-done.5, bf16[256,768]{1,0:T(8,128)(2,1)S(1)} %copy-done.4, ...), custom_call_target="tpu_custom_call" | custom-call | tf_op jit(solution)/shard_map/dft/pallas_call | solution.py:204
  70.8 55.3 %all_to_all.16 = f32[32,128,128]{2,1,0:T(8,128)S(1)} all-to-all(f32[32,128,128]{2,1,0:T(8,128)S(1)} %bitcast.10), channel_id=1, replica_groups={{0,16,32,48,64,80,96,112,128,144,160,176,192,208,224,240,256,272,288,30..., dimensions={0} | all-to-all | bytes 4194304 | tf_op jit(solution)/shard_map/all_to_all | solution.py:330
  126.1 1.0 cross.1
  127.2 35.0 %all_to_all.17.x_ref = f32[16,128,128]{2,1,0:T(8,128)S(1)} all-to-all(f32[16,128,128]{2,1,0:T(8,128)S(1)} %cross.1), channel_id=1, replica_groups={{0,1,2,3,4,5,6,7,8,9,10,11,12,13,14,15},{16,17,18,19,20,21,22,23,24,25,..., dimensions={0} | all-to-all | bytes 2097152 | tf_op jit(solution)/shard_map/all_to_all | solution.py:330
  162.1 0.0 copy-done.9
  162.1 1.6 moments.1
  (3 shorter events, 0.0 us)
Async XLA Ops:
  2.8 65.3 %copy-start = (bf16[512,768]{1,0:T(8,128)(2,1)S(1)}, bf16[512,768]{1,0:T(8,128)(2,1)}, u32[]{:S(2)}) copy-start(bf16[512,768]{1,0:T(8,128)(2,1)} %constant.23.clone.edge_ref) | copy-start | bytes 2359300
  2.8 65.3 %copy-start.1 = (f32[512,256]{1,0:T(8,128)S(1)}, f32[512,256]{1,0:T(8,128)}, u32[]{:S(2)}) copy-start(f32[512,256]{1,0:T(8,128)} %constant.16.clone.w_ref) | copy-start | bytes 1572868
  2.8 65.3 %copy-start.2 = (bf16[256,768]{1,0:T(8,128)(2,1)S(1)}, bf16[256,768]{1,0:T(8,128)(2,1)}, u32[]{:S(2)}) copy-start(bf16[256,768]{1,0:T(8,128)(2,1)} %constant.22.clone.so_ref) | copy-start | bytes 1179652
  2.8 65.3 %copy-start.3 = (bf16[256,768]{1,0:T(8,128)(2,1)S(1)}, bf16[256,768]{1,0:T(8,128)(2,1)}, u32[]{:S(2)}) copy-start(bf16[256,768]{1,0:T(8,128)(2,1)} %constant.21.clone.se_ref) | copy-start | bytes 1179652
  2.8 65.3 %copy-start.4 = (bf16[256,768]{1,0:T(8,128)(2,1)S(1)}, bf16[256,768]{1,0:T(8,128)(2,1)}, u32[]{:S(2)}) copy-start(bf16[256,768]{1,0:T(8,128)(2,1)} %constant.20.clone.fo_ref) | copy-start | bytes 1179652
  2.8 65.3 %copy-start.5 = (bf16[256,768]{1,0:T(8,128)(2,1)S(1)}, bf16[256,768]{1,0:T(8,128)(2,1)}, u32[]{:S(2)}) copy-start(bf16[256,768]{1,0:T(8,128)(2,1)} %constant.19.clone.fe_ref) | copy-start | bytes 1179652
  2.9 65.3 %copy-start.6 = (f32[256,256]{1,0:T(8,128)S(1)}, f32[256,256]{1,0:T(8,128)}, u32[]{:S(2)}) copy-start(f32[256,256]{1,0:T(8,128)} %constant.18.clone.s_ref) | copy-start | bytes 786436
  2.9 65.3 %copy-start.7 = (f32[256,256]{1,0:T(8,128)S(1)}, f32[256,256]{1,0:T(8,128)}, u32[]{:S(2)}) copy-start(f32[256,256]{1,0:T(8,128)} %constant.17.clone.c_ref) | copy-start | bytes 786436
  126.1 36.0 %copy-start.8 = (s32[16]{0:T(128)S(1)}, s32[16]{0:T(128)}, u32[]{:S(2)}) copy-start(s32[16]{0:T(128)} %param.12) | copy-start | bytes 196
  126.1 36.0 %copy-start.9 = (s32[16]{0:T(128)S(1)}, s32[16]{0:T(128)}, u32[]{:S(2)}) copy-start(s32[16]{0:T(128)} %param.13) | copy-start | bytes 196
